TPU v7x, 256 devices: a whole 4x4x8 slice. The times are simulated.
256 devices in a mesh: row: 16 (over y, x), col: 8 (over z), depth: 2 (over core).
Axes of the slice: x: 4, y: 4, z: 8, core: 2. Of those that a mesh axis runs over, the one named last changes fastest.
Arguments:
- ham_blocks: bfloat16 [512, 8, 128, 128], P(('row', 'depth'), 'col'), may hold values from -0.25 to 0.25
- deriv_blocks: bfloat16 [512, 8, 128, 128], P(('row', 'depth'), 'col'), may hold values from -0.25 to 0.25
- ham_cols: int32 [512, 8], P(('row', 'depth')), may hold values from 0 to 511, as said below
- cheb_prev: bfloat16 [32, 64, 128, 128], P('col', 'row'), may hold values from -6 to 6
- cheb_cur: bfloat16 [32, 64, 128, 128], P('col', 'row'), may hold values from -6 to 6
- tang_prev: bfloat16 [32, 64, 128, 128], P('col', 'row'), may hold values from -6 to 6
- tang_cur: bfloat16 [32, 64, 128, 128], P('col', 'row'), may hold values from -6 to 6
- cheb_rows: int32 [32, 64], P('col'), may hold values from 0 to 511, as said below
- keep_mask: int32 [32, 64], P('col', 'row'), may hold values 0 or 1
Outputs:
- cheb_last: bfloat16 [32, 64, 128, 128], P('col', 'row')
- tang_last: bfloat16 [32, 64, 128, 128], P('col', 'row')
Inputs may be any that keep to these rules, and one draw needn't show every extreme that they name: `ham_cols`: each block row lists 8 different block columns, 1 of them in each of the 8 ranges of 64 columns, the ranges in order along the slots. `cheb_rows`: each window column lists 64 different block rows, 2 of them in each of the 32 ranges of 16 rows, the ranges in order along the slots.
All inputs are finite; a program needn't handle non-finite values. No bound on the sum of `keep_mask` on one device may be relied on, other than what follows from the above.
Results may differ from a plain program's by a relative error of at most 0.0042.
Values may be sent and summed in bfloat16 or wider, within the bound.
No kernel may reach another device: no remote copies, remote signals or barrier semaphores. Data moves between devices by JAX's collectives and lax.ppermute only.
A program may use at most 128 MiB of HBM per device.

v0:
```python
import functools

import jax
import jax.numpy as jnp
from jax import lax
from jax.experimental import pallas as pl
from jax.experimental.pallas import tpu as pltpu
from jax.sharding import PartitionSpec as P

ROWS, COLS, CORES = 16, 8, 2
SIDE = 4
CAP = 8
AXES = ("row", "col", "depth")
HBM = pl.BlockSpec(memory_space=pltpu.HBM)
VMEM = pl.BlockSpec(memory_space=pltpu.VMEM)
SMEM = pl.BlockSpec(memory_space=pltpu.SMEM)
ANY = pl.BlockSpec(memory_space=pl.ANY)
HAM_AT, PLACE_AT, OUT_AT, KEEP_AT, COUNT_AT = 0, 64, 128, 192, 200


def side_ring(shift, second):
    pairs = []
    for y in range(SIDE):
        for x in range(SIDE):
            for core in range(CORES):
                along_x = (core == 0) != second
                to_y = y if along_x else (y + shift) % SIDE
                to_x = (x + shift) % SIDE if along_x else x
                pairs.append(((y * SIDE + x) * CORES + core, (to_y * SIDE + to_x) * CORES + core))
    return pairs


def shift_side(array, shift, second):
    return lax.ppermute(array, ("row", "depth"), side_ring(shift, second))


def swap(array):
    return lax.ppermute(array, "depth", [(0, 1), (1, 0)])


def combine_kernel(n_panels, table, ham, *refs):
    panels = refs[:n_panels]
    cheb_old, tang_old, cheb_new, tang_new, ham_buf, panel_buf, acc, sems = refs[n_panels:]

    def issue(entry, carry):
        chunk, i = lax.shift_right_logical(entry, 2), entry & 3
        source = ham.at[table[HAM_AT + entry]]
        pltpu.make_async_copy(source, ham_buf.at[chunk, i], sems.at[0, chunk]).start()
        place = table[PLACE_AT + entry]

        def copy(ref, index):
            pltpu.make_async_copy(ref.at[index], panel_buf.at[chunk, i], sems.at[1, chunk]).start()

        if n_panels == 1:
            copy(panels[0], place)
        else:
            for k, ref in enumerate(panels):
                pl.when(lax.shift_right_logical(place, 3) == k)(functools.partial(copy, ref, place & 7))
        return carry

    lax.fori_loop(0, table[COUNT_AT], issue, 0)
    acc[...] = jnp.zeros_like(acc)
    zero = jnp.zeros((128, 128), jnp.bfloat16)

    def work(chunk, carry):
        pltpu.make_async_copy(ham_buf.at[chunk], ham_buf.at[chunk], sems.at[0, chunk]).wait()
        pltpu.make_async_copy(panel_buf.at[chunk], panel_buf.at[chunk], sems.at[1, chunk]).wait()
        sums = []
        for i in range(4):
            x, t = panel_buf[chunk, i, 0], panel_buf[chunk, i, 1]
            left = jnp.concatenate([ham_buf[chunk, i, 0], ham_buf[chunk, i, 1]], axis=1)
            top = jnp.concatenate([x, t], axis=1)
            right = jnp.concatenate([top, jnp.concatenate([zero, x], axis=1)], axis=0)
            sums.append(jnp.dot(left, right, preferred_element_type=jnp.float32))
        for i in range(4):
            acc[table[OUT_AT + chunk * 4 + i]] += sums[i]
        return carry

    lax.fori_loop(0, lax.shift_right_logical(table[COUNT_AT], 2), work, 0)

    for out in range(8):
        scale = table[KEEP_AT + out].astype(jnp.float32)
        old = cheb_old[out].astype(jnp.float32)
        cheb_new[out] = (scale * (2.0 * acc[out, :, :128] - old)).astype(jnp.bfloat16)
        old = tang_old[out].astype(jnp.float32)
        tang_new[out] = (scale * (2.0 * acc[out, :, 128:] - old)).astype(jnp.bfloat16)


def combine(table, ham, panels, cheb_old, tang_old):
    shape = jax.ShapeDtypeStruct(cheb_old.shape, jnp.bfloat16)
    return pl.pallas_call(
        functools.partial(combine_kernel, len(panels)),
        out_shape=(shape, shape),
        in_specs=[SMEM, HBM] + [ANY] * len(panels) + [VMEM] * 2,
        out_specs=(VMEM, VMEM),
        scratch_shapes=[
            pltpu.VMEM((16, 4, 2, 128, 128), jnp.bfloat16),
            pltpu.VMEM((16, 4, 2, 128, 128), jnp.bfloat16),
            pltpu.VMEM((9, 128, 256), jnp.float32),
            pltpu.SemaphoreType.DMA((2, 16)),
        ],
        compiler_params=pltpu.CompilerParams(vmem_limit_bytes=24 * 1024 * 1024),
        cost_estimate=pl.CostEstimate(flops=1 << 30, bytes_accessed=1 << 23, transcendentals=0),
    )(table, ham, *panels, cheb_old, tang_old)


def pack_kernel(table, *refs):
    panels, packed, sem = refs[:SIDE], refs[SIDE : SIDE + 3], refs[SIDE + 3]

    def copy(ref, index, out, i, slot):
        return pltpu.make_async_copy(ref.at[index], out.at[i], sem.at[slot])

    for wait in (False, True):
        for b, out in enumerate(packed):

            def step(i, carry, b=b, out=out, wait=wait):
                slot = b * CAP + i
                place = table[slot]
                if wait:
                    copy(panels[0], 0, out, i, slot).wait()
                else:
                    for a, ref in enumerate(panels):

                        @pl.when(lax.shift_right_logical(place, 3) == a)
                        def _(ref=ref):
                            copy(ref, place & 7, out, i, slot).start()

                return carry

            lax.fori_loop(0, table[3 * CAP + b], step, 0)


def pack(table, panels):
    shape = jax.ShapeDtypeStruct((CAP, 2, 128, 128), jnp.bfloat16)
    return pl.pallas_call(
        pack_kernel,
        out_shape=(shape,) * 3,
        in_specs=[SMEM] + [ANY] * SIDE,
        out_specs=(VMEM,) * 3,
        scratch_shapes=[pltpu.SemaphoreType.DMA((3 * CAP,))],
        cost_estimate=pl.CostEstimate(flops=0, bytes_accessed=1 << 22, transcendentals=0),
    )(table, *panels)


def position():
    layer, row_group, col = (lax.axis_index(name) for name in ("depth", "row", "col"))
    at_y, at_x = lax.shift_right_logical(row_group, 2), row_group & 3
    return layer, row_group, col, jnp.where(layer == 0, at_x, at_y), jnp.where(layer == 0, at_y, at_x)


def slots_of_rows(rows, layer, slot_of):
    def fill(slot, carry):
        for column in range(2):
            slot_of[column * 512 + rows[2 * layer + column, slot]] = slot
        return carry

    lax.fori_loop(0, 64, fill, 0)


def split(i):
    return lax.shift_right_logical(i, 5), lax.shift_right_logical(i, 3) & 3, i & 7


def coordinates(slot, layer):
    y, x = lax.shift_right_logical(slot, 4), lax.shift_right_logical(slot, 2) & 3
    return jnp.where(layer == 0, x, y), jnp.where(layer == 0, y, x)


def needs_kernel(rows, cols, other_cols, keep, *refs):
    tables, flag, slot_of, counts = refs[:3], refs[3], refs[4], refs[5]
    layer, row_group, col, first, second = position()
    slots_of_rows(rows, layer, slot_of)
    for i in range(5):
        counts[i] = 0

    def put(at, ham, out, places):
        for table, place in zip(tables, places, strict=True):
            table[HAM_AT + at] = ham
            table[OUT_AT + at] = out
            table[PLACE_AT + at] = place

    def look(i, carry):
        column, t, q = split(i)
        group = lax.shift_right_logical(t, 1)
        row = rows[2 * layer + column, 4 * row_group + t] - 32 * row_group - 16 * group
        wanted = jnp.where(group == layer, cols[row, q], other_cols[row, q])
        slot = slot_of[column * 512 + wanted] & 63

        @pl.when((rows[2 * layer + column, slot] == wanted) & (keep[2 * layer + column, t] != 0))
        def _():
            at_first, at_second = coordinates(slot, layer)
            sender = (second - at_second) & 3
            rank = counts[sender]
            counts[sender] = rank + 1
            index = column * 4 + (slot & 3)
            near = ((at_first - first) & 3) * 8 + index
            n = counts[4]
            counts[4] = n + 1
            sparse = jnp.where(sender == 0, near, (sender + 3) * 8 + rank)
            places = (((4 - sender) & 3) * 32 + near, sparse, lax.shift_right_logical(slot, 2) * 8 + index)
            put(n, (q * 2 + group) * 16 + row, lax.shift_right_logical(i, 3), places)

        return carry

    lax.fori_loop(0, 64, look, 0)
    flag[0] = jnp.where((counts[1] > CAP) | (counts[2] > CAP) | (counts[3] > CAP), 1, 0)
    n = counts[4]
    padded = (n + 3) & ~3

    def pad(i, carry):
        put(i, 0, 8, (0, 0, 0))
        return carry

    lax.fori_loop(n, padded, pad, 0)
    for table in tables:
        table[COUNT_AT] = padded
        for out in range(8):
            table[KEEP_AT + out] = keep[2 * layer + out // 4, out % 4]


def needs(cheb_rows, ham_cols, other_cols, keep_mask):
    table = jax.ShapeDtypeStruct((208,), jnp.int32)
    return pl.pallas_call(
        needs_kernel,
        out_shape=(table,) * 3 + (jax.ShapeDtypeStruct((1,), jnp.int32),),
        in_specs=[SMEM] * 4,
        out_specs=(SMEM,) * 4,
        scratch_shapes=[pltpu.SMEM((size,), jnp.int32) for size in (1024, 8)],
    )(cheb_rows, ham_cols, other_cols, keep_mask)


def sends_kernel(rows, *refs):
    known, (table, slot_of, count) = refs[:3], refs[3:]
    layer, row_group, col, first, second = position()
    slots_of_rows(rows, layer, slot_of)
    for b, theirs in enumerate(known):
        to_second = (second + 1 + b) & 3
        to_row = jnp.where(layer == 0, to_second * SIDE + first, first * SIDE + to_second)
        count[0] = 0

        def look(i, carry, b=b, theirs=theirs, to_row=to_row):
            column, t, q = split(i)
            group = lax.shift_right_logical(t, 1)
            row = rows[2 * layer + column, 4 * to_row + t] - 32 * to_row - 16 * group
            wanted = theirs[jnp.where(group == layer, 0, 16) + row, q]
            slot = slot_of[column * 512 + wanted] & 63
            at = (2 * layer + column) * 4 + t
            kept = theirs[32 + lax.shift_right_logical(at, 3), at & 7] != 0
            at_first, at_second = coordinates(slot, layer)

            @pl.when((rows[2 * layer + column, slot] == wanted) & kept & (at_second == second))
            def _():
                rank = count[0]
                count[0] = rank + 1

                @pl.when(rank < CAP)
                def _():
                    table[b * CAP + rank] = ((at_first - first) & 3) * 8 + column * 4 + (slot & 3)

            return carry

        lax.fori_loop(0, 64, look, 0)
        table[3 * CAP + b] = jnp.minimum(count[0], CAP)


def sends(cheb_rows, known):
    return pl.pallas_call(
        sends_kernel,
        out_shape=jax.ShapeDtypeStruct((32,), jnp.int32),
        in_specs=[SMEM] * 4,
        out_specs=SMEM,
        scratch_shapes=[pltpu.SMEM((1024,), jnp.int32), pltpu.SMEM((1,), jnp.int32)],
    )(cheb_rows, *known)


def on_device(
    ham_blocks,
    deriv_blocks,
    ham_cols,
    cheb_prev,
    cheb_cur,
    tang_prev,
    tang_cur,
    cheb_rows,
    keep_mask,
):
    layer = lax.axis_index("depth")

    def mine(array):
        return lax.dynamic_slice_in_dim(array, 2 * layer, 2, 0)

    def own(array):
        return mine(array).reshape(8, 128, 128)

    def paired(cheb, tang):
        return jnp.stack([cheb, tang], axis=1)

    cheb, tang = own(cheb_cur), own(tang_cur)
    ham_pair = jnp.stack([ham_blocks[:, 0], deriv_blocks[:, 0]], axis=1)
    ham = lax.all_gather(ham_pair, ("col", "depth"), axis=0, tiled=True)

    other_cols = swap(ham_cols)
    ring_table, sparse_table, dense_table, overflow = needs(cheb_rows, ham_cols, other_cols, keep_mask)
    flags = lax.all_to_all(jnp.broadcast_to(overflow, (256, 1, 128)), AXES, 0, 0, tiled=True)
    known = jnp.concatenate([ham_cols, other_cols, keep_mask.reshape(2, 8)])
    pack_table = sends(cheb_rows, [shift_side(known, SIDE - b, True) for b in (1, 2, 3)])

    def nearby(piece):
        return [piece] + [shift_side(piece, SIDE - a, False) for a in (1, 2, 3)]

    def ring_panel(piece, ready):
        here = nearby(piece)
        after = [shift_side(piece, SIDE - 1, True) for piece in here]
        before = [shift_side(piece, 1, True) for piece in here]
        last, ready = lax.optimization_barrier((after[0], ready))
        across = [shift_side(piece, SIDE - 1, True) for piece in (last, after[1])]
        across += [shift_side(piece, 1, True) for piece in before[2:]]
        return here + after + across + before, ready

    def sparse_step(ham, cheb, tang, cheb_old, tang_old):
        near_pieces = nearby(paired(cheb, tang))
        packed = pack(pack_table, near_pieces)
        arrived = [shift_side(packed[b - 1], b, True) for b in (1, 2, 3)]
        return combine(sparse_table, ham, near_pieces + arrived, cheb_old, tang_old)

    def dense_step(ham, cheb, tang, cheb_old, tang_old):
        panel = lax.all_gather(paired(cheb, tang), "row", axis=0, tiled=True)
        return combine(dense_table, ham, [panel], cheb_old, tang_old)

    panel, (flags, pack_table) = ring_panel(paired(cheb, tang), (flags, pack_table))
    crowded = jnp.max(flags) > 0
    cheb_mid, tang_mid = combine(ring_table, ham, panel, own(cheb_prev), own(tang_prev))
    cheb_new, tang_new = lax.cond(crowded, dense_step, sparse_step, ham, cheb_mid, tang_mid, cheb, tang)

    def whole(array):
        other = swap(array)
        both = jnp.stack([jnp.where(layer == 0, array, other), jnp.where(layer == 0, other, array)])
        return both.reshape(4, 4, 128, 128)

    return whole(cheb_new), whole(tang_new)


def solution(mesh):
    placed = (
        P(("row", "depth"), "col", None, None),
        P(("row", "depth"), "col", None, None),
        P(("row", "depth"), None),
        P("col", "row", None, None),
        P("col", "row", None, None),
        P("col", "row", None, None),
        P("col", "row", None, None),
        P("col", None),
        P("col", "row"),
    )
    return jax.shard_map(
        on_device,
        mesh=mesh,
        in_specs=placed,
        out_specs=(P("col", "row", None, None), P("col", "row", None, None)),
        check_vma=False,
    )
```

profile of v0, /device:TPU:1, one launch (start us, length us, event | category | flops | bytes accessed | tf_op | source)
XLA Modules:
  0.0 176.7 jit_solution(9637907624923513398)
XLA Ops:
  7.2 2.3 %pad_maximum_fusion.2 = bf16[16,2,128,128]{3,2,1,0:T(8,128)(2,1)} fusion(bf16[16,1,128,128]{3,2,1,0:T(8,128)(2,1)} %param.12, bf16[16,1,128,128]{3,2,1,0:T(8,128)(2,1)} %param.11), kind=kLoop, calls=%fused_computation.2 | loop fusion | flops 524288 | bytes 2097152 | tf_op jit(solution)/shard_map/stack | solution.py:299
  10.3 3.2 %collective-permute-start.7 = (s32[16,8]{1,0:T(8,128)S(1)}, s32[16,8]{1,0:T(8,128)S(1)}, u32[]{:S(2)}, u32[]{:S(2)}) collective-permute-start(s32[16,8]{1,0:T(8,128)S(1)} %copy.22.cols), channel_id=1, source_target_pairs={{0,1},{1,0},{2,3},{3,2},{4,5},{5,4},{6,7},{7,6},{8,9},{9,8},{10,11... | collective-permute-start | bytes 1544 | tf_op jit(solution)/shard_map/ppermute | solution.py:38
  13.6 1.1 constant_dynamic-slice_fusion.2
  15.5 0.8 collective-permute-start.8
  17.5 2.8 %collective-permute-start.11 = (bf16[8,2,128,128]{3,2,1,0:T(8,128)(2,1)S(1)}, bf16[8,2,128,128]{3,2,1,0:T(8,128)(2,1)S(1)}, u32[]{:S(2)}, u32[]{:S(2)}) collective-permute-start(bf16[8,2,128,128]{3,2,1,0:T(8,128)(2,1)S(1)} %pad_maximum_fusion.3.refs_0_), channel_id=1, source_target_pairs={{0,48},{1,193},{16,0},{17,209},{32,16},{33,225},{48,32},{49,241},{... | collective-permute-start | bytes 1572872 | tf_op jit(solution)/shard_map/ppermute | solution.py:34
  21.3 2.1 %collective-permute-start.6 = (bf16[8,2,128,128]{3,2,1,0:T(8,128)(2,1)S(1)}, bf16[8,2,128,128]{3,2,1,0:T(8,128)(2,1)S(1)}, u32[]{:S(2)}, u32[]{:S(2)}) collective-permute-start(bf16[8,2,128,128]{3,2,1,0:T(8,128)(2,1)S(1)} %pad_maximum_fusion.3.refs_0_), channel_id=1, source_target_pairs={{0,192},{1,49},{16,208},{17,1},{32,224},{33,17},{48,240},{49,33},{... | collective-permute-start | bytes 1572872 | tf_op jit(solution)/shard_map/ppermute | solution.py:34
  23.4 6.6 %collective-permute-done.11.refs_1_ = bf16[8,2,128,128]{3,2,1,0:T(8,128)(2,1)S(1)} collective-permute-done((bf16[8,2,128,128]{3,2,1,0:T(8,128)(2,1)S(1)}, bf16[8,2,128,128]{3,2,1,0:T(8,128)(2,1)S(1)}, u32[]{:S(2)}, u32[]{:S(2)}) %collective-permute-start.11) | collective-permute-done | bytes 524320 | tf_op jit(solution)/shard_map/ppermute | solution.py:34
  30.1 2.1 %collective-permute-start.14 = (bf16[8,2,128,128]{3,2,1,0:T(8,128)(2,1)S(1)}, bf16[8,2,128,128]{3,2,1,0:T(8,128)(2,1)}, u32[]{:S(2)}, u32[]{:S(2)}) collective-permute-start(bf16[8,2,128,128]{3,2,1,0:T(8,128)(2,1)S(1)} %collective-permute-done.11.refs_1_), channel_id=1, source_target_pairs={{0,192},{1,49},{16,208},{17,1},{32,224},{33,17},{48,240},{49,33},{... | collective-permute-start | bytes 1572872 | tf_op jit(solution)/shard_map/ppermute | solution.py:34
  32.1 2.0 %collective-permute-start.15 = (bf16[8,2,128,128]{3,2,1,0:T(8,128)(2,1)S(1)}, bf16[8,2,128,128]{3,2,1,0:T(8,128)(2,1)}, u32[]{:S(2)}, u32[]{:S(2)}) collective-permute-start(bf16[8,2,128,128]{3,2,1,0:T(8,128)(2,1)S(1)} %collective-permute-done.12.refs_2_), channel_id=1, source_target_pairs={{0,192},{1,49},{16,208},{17,1},{32,224},{33,17},{48,240},{49,33},{... | collective-permute-start | bytes 1572872 | tf_op jit(solution)/shard_map/ppermute | solution.py:34
  34.2 6.4 %collective-permute-done.13.refs_3_ = bf16[8,2,128,128]{3,2,1,0:T(8,128)(2,1)S(1)} collective-permute-done((bf16[8,2,128,128]{3,2,1,0:T(8,128)(2,1)S(1)}, bf16[8,2,128,128]{3,2,1,0:T(8,128)(2,1)S(1)}, u32[]{:S(2)}, u32[]{:S(2)}) %collective-permute-start.13) | collective-permute-done | bytes 524320 | tf_op jit(solution)/shard_map/ppermute | solution.py:34
  40.6 2.1 %collective-permute-start.16 = (bf16[8,2,128,128]{3,2,1,0:T(8,128)(2,1)S(1)}, bf16[8,2,128,128]{3,2,1,0:T(8,128)(2,1)}, u32[]{:S(2)}, u32[]{:S(2)}) collective-permute-start(bf16[8,2,128,128]{3,2,1,0:T(8,128)(2,1)S(1)} %collective-permute-done.13.refs_3_), channel_id=1, source_target_pairs={{0,192},{1,49},{16,208},{17,1},{32,224},{33,17},{48,240},{49,33},{... | collective-permute-start | bytes 1572872 | tf_op jit(solution)/shard_map/ppermute | solution.py:34
  43.2 0.8 copy-done.9
  44.4 4.9 %shard_map.104 = (s32[208]{0:T(256)}, s32[208]{0:T(256)S(1)}, s32[208]{0:T(256)S(1)}, s32[1]{0:T(128)}) custom-call(s32[4,64]{1,0:T(4,128)} %rows.3, s32[16,8]{1,0:T(8,128)} %copy-done.13, s32[16,8]{1,0:T(8,128)} %copy-done.14, s32[4,4]{1,0:T(4,128)} %keep.1), custom_call_target="tpu_custom_call" | custom-call | tf_op jit(solution)/shard_map/pallas_call | solution.py:223
  49.3 1.3 broadcast_in_dim.2
  50.6 17.4 %all-to-all-start = ((s32[256,1,128]{2,1,0:T(1,128)}), s32[256,1,128]{2,1,0:T(1,128)S(1)}, u32[]{:S(2)}, u32[]{:S(2)}) async-start(s32[256,1,128]{2,1,0:T(1,128)} %broadcast_in_dim.2), calls=%async_computation | async-start | bytes 262144 | tf_op jit(solution)/shard_map/all_to_all | solution.py:304
  68.1 9.2 %shard_map.105 = s32[32]{0:T(128)S(1)} custom-call(s32[4,64]{1,0:T(4,128)} %rows.3, s32[34,8]{1,0:T(8,128)} %copy-done.15, s32[34,8]{1,0:T(8,128)} %copy-done.16, s32[34,8]{1,0:T(8,128)} %copy-done.17), custom_call_target="tpu_custom_call" | custom-call | tf_op jit(solution)/shard_map/pallas_call | solution.py:267
  77.3 5.1 %all-to-all-done = s32[256,1,128]{2,1,0:T(1,128)S(1)} async-done(((s32[256,1,128]{2,1,0:T(1,128)}), s32[256,1,128]{2,1,0:T(1,128)S(1)}, u32[]{:S(2)}, u32[]{:S(2)}) %all-to-all-start) | async-done | bytes 131104 | tf_op jit(solution)/shard_map/all_to_all | solution.py:304
  82.8 1.1 collective-permute-start.24
  84.0 1.5 collective-permute-start.18
  85.6 1.1 constant_dynamic-slice_fusion
  86.7 0.9 reduce_max.9
  88.2 2.7 %collective-permute-done.17.refs_8_ = bf16[8,2,128,128]{3,2,1,0:T(8,128)(2,1)} collective-permute-done((bf16[8,2,128,128]{3,2,1,0:T(8,128)(2,1)S(1)}, bf16[8,2,128,128]{3,2,1,0:T(8,128)(2,1)}, u32[]{:S(2)}, u32[]{:S(2)}) %collective-permute-start.17) | collective-permute-done | bytes 524320 | tf_op jit(solution)/shard_map/ppermute | solution.py:34
  90.9 1.5 collective-permute-done.24.refs_13_
  92.5 4.1 %collective-permute-done.18.refs_9_ = bf16[8,2,128,128]{3,2,1,0:T(8,128)(2,1)} collective-permute-done((bf16[8,2,128,128]{3,2,1,0:T(8,128)(2,1)}, bf16[8,2,128,128]{3,2,1,0:T(8,128)(2,1)}, u32[]{:S(2)}, u32[]{:S(2)}) %collective-permute-start.18) | collective-permute-done | bytes 524320 | tf_op jit(solution)/shard_map/ppermute | solution.py:34
  96.5 1.5 collective-permute-done.20.refs_10_
  98.1 5.6 %collective-permute-done.22.refs_11_ = bf16[8,2,128,128]{3,2,1,0:T(8,128)(2,1)} collective-permute-done((bf16[8,2,128,128]{3,2,1,0:T(8,128)(2,1)}, bf16[8,2,128,128]{3,2,1,0:T(8,128)(2,1)}, u32[]{:S(2)}, u32[]{:S(2)}) %collective-permute-start.22) | collective-permute-done | bytes 524320 | tf_op jit(solution)/shard_map/ppermute | solution.py:34
  103.7 8.6 %all-gather.5.cloned.1.call-done.ham = bf16[256,2,128,128]{3,2,1,0:T(8,128)(2,1)} async-done(((bf16[16,2,128,128]{3,2,1,0:T(8,128)(2,1)}), bf16[256,2,128,128]{3,2,1,0:T(8,128)(2,1)}) %all-gather.5.cloned.1.call-update) | async-done | bytes 16777232 | tf_op jit(solution)/shard_map/all_gather | solution.py:300
  112.3 1.0 copy-done.10
  114.0 3.6 %shard_map.106 = (bf16[8,128,128]{2,1,0:T(8,128)(2,1)}, bf16[8,128,128]{2,1,0:T(8,128)(2,1)}) custom-call(s32[208]{0:T(256)S(1)} %copy-done.11, bf16[256,2,128,128]{3,2,1,0:T(8,128)(2,1)} %all-gather.5.cloned.1.call-done.ham, bf16[8,2,128,128]{3,2,1,0:T(8,128)(2,1)S(1)} %pad_maximum_fusion.3.refs_0_, ...), custom_call_target="tpu_custom_call" | custom-call | flops 1073741824 | bytes 8388608 | tf_op jit(solution)/shard_map/pallas_call | solution.py:91
  117.6 47.2 %conditional.1 = ((bf16[8,128,128]{2,1,0:T(8,128)(2,1)S(1)}, bf16[8,128,128]{2,1,0:T(8,128)(2,1)S(1)})) conditional(s32[]{:T(128)} %convert_element_type.3, (bf16[8,128,128]{2,1,0:T(8,128)(2,1)}, bf16[8,128,128]{2,1,0:T(8,128)(2,1)}, s32[32]{0:T(128)S(1)}, s32[208]{0:T(256)S(1)}, bf16[256,2,128,128]{3,2,1,0:T(8,128)(2,1)}, ...), branch_computations={%region_1.0_spmd, %region_2.0_spmd} | conditional | flops 1074003968 | bytes 69730376 | solution.py:333
  117.6 1.1 pad_maximum_fusion.refs_0_
  118.7 3.6 %collective-permute-start = (bf16[8,2,128,128]{3,2,1,0:T(8,128)(2,1)S(1)}, bf16[8,2,128,128]{3,2,1,0:T(8,128)(2,1)S(1)}, u32[]{:S(2)}, u32[]{:S(2)}) collective-permute-start(bf16[8,2,128,128]{3,2,1,0:T(8,128)(2,1)S(1)} %pad_maximum_fusion.refs_0_), channel_id=1, source_target_pairs={{0,48},{1,193},{16,0},{17,209},{32,16},{33,225},{48,32},{49,241},{... | collective-permute-start | bytes 1572872 | tf_op jit(solution)/shard_map/cond/branch_0_fun/ppermute | solution.py:34
  123.0 11.1 %collective-permute-done.refs_1_ = bf16[8,2,128,128]{3,2,1,0:T(8,128)(2,1)S(1)} collective-permute-done((bf16[8,2,128,128]{3,2,1,0:T(8,128)(2,1)S(1)}, bf16[8,2,128,128]{3,2,1,0:T(8,128)(2,1)S(1)}, u32[]{:S(2)}, u32[]{:S(2)}) %collective-permute-start) | collective-permute-done | bytes 524320 | tf_op jit(solution)/shard_map/cond/branch_0_fun/ppermute | solution.py:34
  134.1 3.2 %collective-permute-done.2.refs_3_ = bf16[8,2,128,128]{3,2,1,0:T(8,128)(2,1)S(1)} collective-permute-done((bf16[8,2,128,128]{3,2,1,0:T(8,128)(2,1)S(1)}, bf16[8,2,128,128]{3,2,1,0:T(8,128)(2,1)S(1)}, u32[]{:S(2)}, u32[]{:S(2)}) %collective-permute-start.2) | collective-permute-done | bytes 524320 | tf_op jit(solution)/shard_map/cond/branch_0_fun/ppermute | solution.py:34
  137.3 0.8 copy-done.7
  138.1 3.0 %branch_0_fun.2 = (bf16[8,2,128,128]{3,2,1,0:T(8,128)(2,1)}, bf16[8,2,128,128]{3,2,1,0:T(8,128)(2,1)}, bf16[8,2,128,128]{3,2,1,0:T(8,128)(2,1)}) custom-call(s32[32]{0:T(128)S(1)} %get-tuple-element.30.table, bf16[8,2,128,128]{3,2,1,0:T(8,128)(2,1)} %copy-done.1, bf16[8,2,128,128]{3,2,1,0:T(8,128)(2,1)} %copy-done.3, bf16[8,2,128,128]{3,2,1,0:T(8,128)(2,1)} %copy-done.5, ...), custom_call_target="tpu_custom_call" | custom-call | bytes 4194304 | tf_op jit(solution)/shard_map/cond/branch_0_fun/pallas_call | solution.py:135
  141.3 2.4 %collective-permute-start.4 = (bf16[8,2,128,128]{3,2,1,0:T(8,128)(2,1)}, bf16[8,2,128,128]{3,2,1,0:T(8,128)(2,1)S(1)}, u32[]{:S(2)}, u32[]{:S(2)}) collective-permute-start(bf16[8,2,128,128]{3,2,1,0:T(8,128)(2,1)} %get-tuple-element.32), channel_id=1, source_target_pairs={{0,128},{1,33},{16,144},{17,49},{32,160},{33,1},{48,176},{49,17},{... | collective-permute-start | bytes 1572872 | tf_op jit(solution)/shard_map/cond/branch_0_fun/ppermute | solution.py:34
  143.7 1.4 collective-permute-start.5
  145.0 11.5 %collective-permute-done.3.refs_4_ = bf16[8,2,128,128]{3,2,1,0:T(8,128)(2,1)S(1)} collective-permute-done((bf16[8,2,128,128]{3,2,1,0:T(8,128)(2,1)}, bf16[8,2,128,128]{3,2,1,0:T(8,128)(2,1)S(1)}, u32[]{:S(2)}, u32[]{:S(2)}) %collective-permute-start.3) | collective-permute-done | bytes 524320 | tf_op jit(solution)/shard_map/cond/branch_0_fun/ppermute | solution.py:34
  157.1 1.0 copy-done.2
  158.2 1.0 copy-done.4
  159.2 1.0 copy-done.6
  160.3 1.0 copy-done.8
  161.3 3.5 %branch_0_fun.3 = (bf16[8,128,128]{2,1,0:T(8,128)(2,1)S(1)}, bf16[8,128,128]{2,1,0:T(8,128)(2,1)S(1)}) custom-call(s32[208]{0:T(256)S(1)} %get-tuple-element.26.table, bf16[256,2,128,128]{3,2,1,0:T(8,128)(2,1)} %get-tuple-element.27.ham, bf16[8,2,128,128]{3,2,1,0:T(8,128)(2,1)S(1)} %copy-done.2, bf16[8,2,128,128]{3,2,1,0:T(8,128)(2,1)S(1)} %copy-done.4, ...), custom_call_target="tpu_custom_call" | custom-call | flops 1073741824 | bytes 8388608 | tf_op jit(solution)/shard_map/cond/branch_0_fun/pallas_call | solution.py:91
  164.8 2.1 %collective-permute-start.25 = (bf16[8,128,128]{2,1,0:T(8,128)(2,1)S(1)}, bf16[8,128,128]{2,1,0:T(8,128)(2,1)S(1)}, u32[]{:S(2)}, u32[]{:S(2)}) collective-permute-start(bf16[8,128,128]{2,1,0:T(8,128)(2,1)S(1)} %get-tuple-element.64), channel_id=1, source_target_pairs={{0,1},{1,0},{2,3},{3,2},{4,5},{5,4},{6,7},{7,6},{8,9},{9,8},{10,11... | collective-permute-start | bytes 786440 | tf_op jit(solution)/shard_map/ppermute | solution.py:38
  167.0 1.1 collective-permute-done.25
  168.1 0.8 pad_maximum_fusion.4
  169.0 0.8 pad_maximum_fusion.5
  (65 shorter events, 7.5 us)
Async XLA Ops:
  7.2 105.1 %all-gather.5.cloned.1.call-start = ((), (), s32[]{:S(2)}) async-start(), calls=%async_computation.2 | async-start | bytes 17825792 | tf_op jit(solution)/shard_map/all_gather | solution.py:300
  10.3 34.1 %copy-start.13 = (s32[16,8]{1,0:T(8,128)}, s32[16,8]{1,0:T(8,128)S(1)}, u32[]{:S(2)}) copy-start(s32[16,8]{1,0:T(8,128)S(1)} %copy.22.cols) | copy-start | bytes 1540
  10.3 5.1 %collective-permute-start.7 = (s32[16,8]{1,0:T(8,128)S(1)}, s32[16,8]{1,0:T(8,128)S(1)}, u32[]{:S(2)}, u32[]{:S(2)}) collective-permute-start(s32[16,8]{1,0:T(8,128)S(1)} %copy.22.cols), channel_id=1, source_target_pairs={{0,1},{1,0},{2,3},{3,2},{4,5},{5,4},{6,7},{7,6},{8,9},{9,8},{10,11... | collective-permute-start | bytes 1544 | tf_op jit(solution)/shard_map/ppermute | solution.py:38
  14.6 2.8 %copy-start.12 = (bf16[2,4,128,128]{3,2,1,0:T(8,128)(2,1)}, bf16[2,4,128,128]{3,2,1,0:T(8,128)(2,1)S(1)}, u32[]{:S(2)}) copy-start(bf16[2,4,128,128]{3,2,1,0:T(8,128)(2,1)S(1)} %get-tuple-element.73) | copy-start | bytes 786436
  15.5 28.9 %copy-start.14 = (s32[16,8]{1,0:T(8,128)}, s32[16,8]{1,0:T(8,128)S(1)}, u32[]{:S(2)}) copy-start(s32[16,8]{1,0:T(8,128)S(1)} %collective-permute-done.7.other_cols) | copy-start | bytes 1540
  15.5 5.2 %collective-permute-start.8 = (s32[34,8]{1,0:T(8,128)S(1)}, s32[34,8]{1,0:T(8,128)S(1)}, u32[]{:S(2)}, u32[]{:S(2)}) collective-permute-start(s32[34,8]{1,0:T(8,128)S(1)} %pad_add_fusion), channel_id=1, source_target_pairs={{0,192},{1,49},{16,208},{17,1},{32,224},{33,17},{48,240},{49,33},{... | collective-permute-start | bytes 3272 | tf_op jit(solution)/shard_map/ppermute | solution.py:34
  16.3 5.0 %collective-permute-start.9 = (s32[34,8]{1,0:T(8,128)S(1)}, s32[34,8]{1,0:T(8,128)S(1)}, u32[]{:S(2)}, u32[]{:S(2)}) collective-permute-start(s32[34,8]{1,0:T(8,128)S(1)} %pad_add_fusion), channel_id=1, source_target_pairs={{0,128},{1,33},{16,144},{17,49},{32,160},{33,1},{48,176},{49,17},{... | collective-permute-start | bytes 3272 | tf_op jit(solution)/shard_map/ppermute | solution.py:34
  16.8 6.6 %collective-permute-start.10 = (s32[34,8]{1,0:T(8,128)S(1)}, s32[34,8]{1,0:T(8,128)S(1)}, u32[]{:S(2)}, u32[]{:S(2)}) collective-permute-start(s32[34,8]{1,0:T(8,128)S(1)} %pad_add_fusion), channel_id=1, source_target_pairs={{0,64},{1,17},{16,80},{17,33},{32,96},{33,49},{48,112},{49,1},{64,... | collective-permute-start | bytes 3272 | tf_op jit(solution)/shard_map/ppermute | solution.py:34
  17.5 12.6 %collective-permute-start.11 = (bf16[8,2,128,128]{3,2,1,0:T(8,128)(2,1)S(1)}, bf16[8,2,128,128]{3,2,1,0:T(8,128)(2,1)S(1)}, u32[]{:S(2)}, u32[]{:S(2)}) collective-permute-start(bf16[8,2,128,128]{3,2,1,0:T(8,128)(2,1)S(1)} %pad_maximum_fusion.3.refs_0_), channel_id=1, source_target_pairs={{0,48},{1,193},{16,0},{17,209},{32,16},{33,225},{48,32},{49,241},{... | collective-permute-start | bytes 1572872 | tf_op jit(solution)/shard_map/ppermute | solution.py:34
  20.3 11.9 %collective-permute-start.12 = (bf16[8,2,128,128]{3,2,1,0:T(8,128)(2,1)S(1)}, bf16[8,2,128,128]{3,2,1,0:T(8,128)(2,1)S(1)}, u32[]{:S(2)}, u32[]{:S(2)}) collective-permute-start(bf16[8,2,128,128]{3,2,1,0:T(8,128)(2,1)S(1)} %pad_maximum_fusion.3.refs_0_), channel_id=1, source_target_pairs={{0,32},{1,129},{16,48},{17,145},{32,0},{33,161},{48,16},{49,177},{... | collective-permute-start | bytes 1572872 | tf_op jit(solution)/shard_map/ppermute | solution.py:34
  20.6 47.4 %copy-start.15 = (s32[34,8]{1,0:T(8,128)}, s32[34,8]{1,0:T(8,128)S(1)}, u32[]{:S(2)}) copy-start(s32[34,8]{1,0:T(8,128)S(1)} %collective-permute-done.8.refs_0_) | copy-start | bytes 3268
  20.6 20.0 %collective-permute-start.13 = (bf16[8,2,128,128]{3,2,1,0:T(8,128)(2,1)S(1)}, bf16[8,2,128,128]{3,2,1,0:T(8,128)(2,1)S(1)}, u32[]{:S(2)}, u32[]{:S(2)}) collective-permute-start(bf16[8,2,128,128]{3,2,1,0:T(8,128)(2,1)S(1)} %pad_maximum_fusion.3.refs_0_), channel_id=1, source_target_pairs={{0,16},{1,65},{16,32},{17,81},{32,48},{33,97},{48,0},{49,113},{64,... | collective-permute-start | bytes 1572872 | tf_op jit(solution)/shard_map/ppermute | solution.py:34
  21.3 46.8 %copy-start.16 = (s32[34,8]{1,0:T(8,128)}, s32[34,8]{1,0:T(8,128)S(1)}, u32[]{:S(2)}) copy-start(s32[34,8]{1,0:T(8,128)S(1)} %collective-permute-done.9.refs_1_) | copy-start | bytes 3268
  21.3 21.3 %collective-permute-start.6 = (bf16[8,2,128,128]{3,2,1,0:T(8,128)(2,1)S(1)}, bf16[8,2,128,128]{3,2,1,0:T(8,128)(2,1)S(1)}, u32[]{:S(2)}, u32[]{:S(2)}) collective-permute-start(bf16[8,2,128,128]{3,2,1,0:T(8,128)(2,1)S(1)} %pad_maximum_fusion.3.refs_0_), channel_id=1, source_target_pairs={{0,192},{1,49},{16,208},{17,1},{32,224},{33,17},{48,240},{49,33},{... | collective-permute-start | bytes 1572872 | tf_op jit(solution)/shard_map/ppermute | solution.py:34
  23.4 44.7 %copy-start.17 = (s32[34,8]{1,0:T(8,128)}, s32[34,8]{1,0:T(8,128)S(1)}, u32[]{:S(2)}) copy-start(s32[34,8]{1,0:T(8,128)S(1)} %collective-permute-done.10.refs_2_) | copy-start | bytes 3268
  23.4 19.8 %collective-permute-start.23 = (bf16[8,2,128,128]{3,2,1,0:T(8,128)(2,1)S(1)}, bf16[8,2,128,128]{3,2,1,0:T(8,128)(2,1)S(1)}, u32[]{:S(2)}, u32[]{:S(2)}) collective-permute-start(bf16[8,2,128,128]{3,2,1,0:T(8,128)(2,1)S(1)} %pad_maximum_fusion.3.refs_0_), channel_id=1, source_target_pairs={{0,64},{1,17},{16,80},{17,33},{32,96},{33,49},{48,112},{49,1},{64,... | collective-permute-start | bytes 1572872 | tf_op jit(solution)/shard_map/ppermute | solution.py:34
  30.1 52.4 %collective-permute-start.14 = (bf16[8,2,128,128]{3,2,1,0:T(8,128)(2,1)S(1)}, bf16[8,2,128,128]{3,2,1,0:T(8,128)(2,1)}, u32[]{:S(2)}, u32[]{:S(2)}) collective-permute-start(bf16[8,2,128,128]{3,2,1,0:T(8,128)(2,1)S(1)} %collective-permute-done.11.refs_1_), channel_id=1, source_target_pairs={{0,192},{1,49},{16,208},{17,1},{32,224},{33,17},{48,240},{49,33},{... | collective-permute-start | bytes 1572872 | tf_op jit(solution)/shard_map/ppermute | solution.py:34
  32.1 50.7 %collective-permute-start.15 = (bf16[8,2,128,128]{3,2,1,0:T(8,128)(2,1)S(1)}, bf16[8,2,128,128]{3,2,1,0:T(8,128)(2,1)}, u32[]{:S(2)}, u32[]{:S(2)}) collective-permute-start(bf16[8,2,128,128]{3,2,1,0:T(8,128)(2,1)S(1)} %collective-permute-done.12.refs_2_), channel_id=1, source_target_pairs={{0,192},{1,49},{16,208},{17,1},{32,224},{33,17},{48,240},{49,33},{... | collective-permute-start | bytes 1572872 | tf_op jit(solution)/shard_map/ppermute | solution.py:34
  40.6 43.4 %collective-permute-start.16 = (bf16[8,2,128,128]{3,2,1,0:T(8,128)(2,1)S(1)}, bf16[8,2,128,128]{3,2,1,0:T(8,128)(2,1)}, u32[]{:S(2)}, u32[]{:S(2)}) collective-permute-start(bf16[8,2,128,128]{3,2,1,0:T(8,128)(2,1)S(1)} %collective-permute-done.13.refs_3_), channel_id=1, source_target_pairs={{0,192},{1,49},{16,208},{17,1},{32,224},{33,17},{48,240},{49,33},{... | collective-permute-start | bytes 1572872 | tf_op jit(solution)/shard_map/ppermute | solution.py:34
  42.7 42.8 %collective-permute-start.19 = (bf16[8,2,128,128]{3,2,1,0:T(8,128)(2,1)S(1)}, bf16[8,2,128,128]{3,2,1,0:T(8,128)(2,1)}, u32[]{:S(2)}, u32[]{:S(2)}) collective-permute-start(bf16[8,2,128,128]{3,2,1,0:T(8,128)(2,1)S(1)} %collective-permute-done.12.refs_2_), channel_id=1, source_target_pairs={{0,64},{1,17},{16,80},{17,33},{32,96},{33,49},{48,112},{49,1},{64,... | collective-permute-start | bytes 1572872 | tf_op jit(solution)/shard_map/ppermute | solution.py:34
  43.2 0.8 copy-start.9
  44.0 41.5 %collective-permute-start.21 = (bf16[8,2,128,128]{3,2,1,0:T(8,128)(2,1)S(1)}, bf16[8,2,128,128]{3,2,1,0:T(8,128)(2,1)}, u32[]{:S(2)}, u32[]{:S(2)}) collective-permute-start(bf16[8,2,128,128]{3,2,1,0:T(8,128)(2,1)S(1)} %collective-permute-done.13.refs_3_), channel_id=1, source_target_pairs={{0,64},{1,17},{16,80},{17,33},{32,96},{33,49},{48,112},{49,1},{64,... | collective-permute-start | bytes 1572872 | tf_op jit(solution)/shard_map/ppermute | solution.py:34
  50.6 31.8 %all-to-all-start = ((s32[256,1,128]{2,1,0:T(1,128)}), s32[256,1,128]{2,1,0:T(1,128)S(1)}, u32[]{:S(2)}, u32[]{:S(2)}) async-start(s32[256,1,128]{2,1,0:T(1,128)} %broadcast_in_dim.2), calls=%async_computation | async-start | bytes 262144 | tf_op jit(solution)/shard_map/all_to_all | solution.py:304
  82.5 8.4 %collective-permute-start.17 = (bf16[8,2,128,128]{3,2,1,0:T(8,128)(2,1)S(1)}, bf16[8,2,128,128]{3,2,1,0:T(8,128)(2,1)}, u32[]{:S(2)}, u32[]{:S(2)}) collective-permute-start(bf16[8,2,128,128]{3,2,1,0:T(8,128)(2,1)S(1)} %collective-permute-done.6.refs_4_), channel_id=1, source_target_pairs={{0,192},{1,49},{16,208},{17,1},{32,224},{33,17},{48,240},{49,33},{... | collective-permute-start | bytes 1572872 | tf_op jit(solution)/shard_map/ppermute | solution.py:34
  82.8 9.6 %collective-permute-start.24 = (bf16[8,2,128,128]{3,2,1,0:T(8,128)(2,1)S(1)}, bf16[8,2,128,128]{3,2,1,0:T(8,128)(2,1)}, u32[]{:S(2)}, u32[]{:S(2)}) collective-permute-start(bf16[8,2,128,128]{3,2,1,0:T(8,128)(2,1)S(1)} %collective-permute-done.11.refs_1_), channel_id=1, source_target_pairs={{0,64},{1,17},{16,80},{17,33},{32,96},{33,49},{48,112},{49,1},{64,... | collective-permute-start | bytes 1572872 | tf_op jit(solution)/shard_map/ppermute | solution.py:34
  84.0 12.6 %collective-permute-start.18 = (bf16[8,2,128,128]{3,2,1,0:T(8,128)(2,1)}, bf16[8,2,128,128]{3,2,1,0:T(8,128)(2,1)}, u32[]{:S(2)}, u32[]{:S(2)}) collective-permute-start(bf16[8,2,128,128]{3,2,1,0:T(8,128)(2,1)} %collective-permute-done.14.refs_5_), channel_id=1, source_target_pairs={{0,192},{1,49},{16,208},{17,1},{32,224},{33,17},{48,240},{49,33},{... | collective-permute-start | bytes 1572872 | tf_op jit(solution)/shard_map/ppermute | solution.py:34
  85.5 12.6 %collective-permute-start.20 = (bf16[8,2,128,128]{3,2,1,0:T(8,128)(2,1)}, bf16[8,2,128,128]{3,2,1,0:T(8,128)(2,1)}, u32[]{:S(2)}, u32[]{:S(2)}) collective-permute-start(bf16[8,2,128,128]{3,2,1,0:T(8,128)(2,1)} %collective-permute-done.19.refs_14_), channel_id=1, source_target_pairs={{0,64},{1,17},{16,80},{17,33},{32,96},{33,49},{48,112},{49,1},{64,... | collective-permute-start | bytes 1572872 | tf_op jit(solution)/shard_map/ppermute | solution.py:34
  85.5 18.2 %collective-permute-start.22 = (bf16[8,2,128,128]{3,2,1,0:T(8,128)(2,1)}, bf16[8,2,128,128]{3,2,1,0:T(8,128)(2,1)}, u32[]{:S(2)}, u32[]{:S(2)}) collective-permute-start(bf16[8,2,128,128]{3,2,1,0:T(8,128)(2,1)} %collective-permute-done.21.refs_15_), channel_id=1, source_target_pairs={{0,64},{1,17},{16,80},{17,33},{32,96},{33,49},{48,112},{49,1},{64,... | collective-permute-start | bytes 1572872 | tf_op jit(solution)/shard_map/ppermute | solution.py:34
  112.3 1.0 copy-start.10
  113.3 0.6 copy-start.11
  118.7 18.6 %copy-start.1 = (bf16[8,2,128,128]{3,2,1,0:T(8,128)(2,1)}, bf16[8,2,128,128]{3,2,1,0:T(8,128)(2,1)S(1)}, u32[]{:S(2)}) copy-start(bf16[8,2,128,128]{3,2,1,0:T(8,128)(2,1)S(1)} %pad_maximum_fusion.refs_0_) | copy-start | bytes 1572868 | tf_op jit(solution)/shard_map/cond
  118.7 15.4 %collective-permute-start = (bf16[8,2,128,128]{3,2,1,0:T(8,128)(2,1)S(1)}, bf16[8,2,128,128]{3,2,1,0:T(8,128)(2,1)S(1)}, u32[]{:S(2)}, u32[]{:S(2)}) collective-permute-start(bf16[8,2,128,128]{3,2,1,0:T(8,128)(2,1)S(1)} %pad_maximum_fusion.refs_0_), channel_id=1, source_target_pairs={{0,48},{1,193},{16,0},{17,209},{32,16},{33,225},{48,32},{49,241},{... | collective-permute-start | bytes 1572872 | tf_op jit(solution)/shard_map/cond/branch_0_fun/ppermute | solution.py:34
  122.3 11.7 %collective-permute-start.1 = (bf16[8,2,128,128]{3,2,1,0:T(8,128)(2,1)S(1)}, bf16[8,2,128,128]{3,2,1,0:T(8,128)(2,1)S(1)}, u32[]{:S(2)}, u32[]{:S(2)}) collective-permute-start(bf16[8,2,128,128]{3,2,1,0:T(8,128)(2,1)S(1)} %pad_maximum_fusion.refs_0_), channel_id=1, source_target_pairs={{0,32},{1,129},{16,48},{17,145},{32,0},{33,161},{48,16},{49,177},{... | collective-permute-start | bytes 1572872 | tf_op jit(solution)/shard_map/cond/branch_0_fun/ppermute | solution.py:34
  122.3 15.0 %collective-permute-start.2 = (bf16[8,2,128,128]{3,2,1,0:T(8,128)(2,1)S(1)}, bf16[8,2,128,128]{3,2,1,0:T(8,128)(2,1)S(1)}, u32[]{:S(2)}, u32[]{:S(2)}) collective-permute-start(bf16[8,2,128,128]{3,2,1,0:T(8,128)(2,1)S(1)} %pad_maximum_fusion.refs_0_), channel_id=1, source_target_pairs={{0,16},{1,65},{16,32},{17,81},{32,48},{33,97},{48,0},{49,113},{64,... | collective-permute-start | bytes 1572872 | tf_op jit(solution)/shard_map/cond/branch_0_fun/ppermute | solution.py:34
  134.0 3.2 %copy-start.3 = (bf16[8,2,128,128]{3,2,1,0:T(8,128)(2,1)}, bf16[8,2,128,128]{3,2,1,0:T(8,128)(2,1)S(1)}, u32[]{:S(2)}) copy-start(bf16[8,2,128,128]{3,2,1,0:T(8,128)(2,1)S(1)} %collective-permute-done.refs_1_) | copy-start | bytes 1572868 | tf_op jit(solution)/shard_map/cond
  134.1 3.2 %copy-start.5 = (bf16[8,2,128,128]{3,2,1,0:T(8,128)(2,1)}, bf16[8,2,128,128]{3,2,1,0:T(8,128)(2,1)S(1)}, u32[]{:S(2)}) copy-start(bf16[8,2,128,128]{3,2,1,0:T(8,128)(2,1)S(1)} %collective-permute-done.1.refs_2_) | copy-start | bytes 1572868 | tf_op jit(solution)/shard_map/cond
  137.3 0.8 copy-start.7
  141.1 15.4 %collective-permute-start.3 = (bf16[8,2,128,128]{3,2,1,0:T(8,128)(2,1)}, bf16[8,2,128,128]{3,2,1,0:T(8,128)(2,1)S(1)}, u32[]{:S(2)}, u32[]{:S(2)}) collective-permute-start(bf16[8,2,128,128]{3,2,1,0:T(8,128)(2,1)} %get-tuple-element.31), channel_id=1, source_target_pairs={{0,64},{1,17},{16,80},{17,33},{32,96},{33,49},{48,112},{49,1},{64,... | collective-permute-start | bytes 1572872 | tf_op jit(solution)/shard_map/cond/branch_0_fun/ppermute | solution.py:34
  141.3 15.3 %collective-permute-start.4 = (bf16[8,2,128,128]{3,2,1,0:T(8,128)(2,1)}, bf16[8,2,128,128]{3,2,1,0:T(8,128)(2,1)S(1)}, u32[]{:S(2)}, u32[]{:S(2)}) collective-permute-start(bf16[8,2,128,128]{3,2,1,0:T(8,128)(2,1)} %get-tuple-element.32), channel_id=1, source_target_pairs={{0,128},{1,33},{16,144},{17,49},{32,160},{33,1},{48,176},{49,17},{... | collective-permute-start | bytes 1572872 | tf_op jit(solution)/shard_map/cond/branch_0_fun/ppermute | solution.py:34
  143.7 13.5 %collective-permute-start.5 = (bf16[8,2,128,128]{3,2,1,0:T(8,128)(2,1)}, bf16[8,2,128,128]{3,2,1,0:T(8,128)(2,1)S(1)}, u32[]{:S(2)}, u32[]{:S(2)}) collective-permute-start(bf16[8,2,128,128]{3,2,1,0:T(8,128)(2,1)} %get-tuple-element.33), channel_id=1, source_target_pairs={{0,192},{1,49},{16,208},{17,1},{32,224},{33,17},{48,240},{49,33},{... | collective-permute-start | bytes 1572872 | tf_op jit(solution)/shard_map/cond/branch_0_fun/ppermute | solution.py:34
  157.1 1.0 copy-start.2
  158.2 1.0 copy-start.4
  159.2 1.0 copy-start.6
  160.3 1.0 copy-start.8
  164.8 3.3 %collective-permute-start.25 = (bf16[8,128,128]{2,1,0:T(8,128)(2,1)S(1)}, bf16[8,128,128]{2,1,0:T(8,128)(2,1)S(1)}, u32[]{:S(2)}, u32[]{:S(2)}) collective-permute-start(bf16[8,128,128]{2,1,0:T(8,128)(2,1)S(1)} %get-tuple-element.64), channel_id=1, source_target_pairs={{0,1},{1,0},{2,3},{3,2},{4,5},{5,4},{6,7},{7,6},{8,9},{9,8},{10,11... | collective-permute-start | bytes 786440 | tf_op jit(solution)/shard_map/ppermute | solution.py:38
  166.9 2.0 %collective-permute-start.26 = (bf16[8,128,128]{2,1,0:T(8,128)(2,1)S(1)}, bf16[8,128,128]{2,1,0:T(8,128)(2,1)S(1)}, u32[]{:S(2)}, u32[]{:S(2)}) collective-permute-start(bf16[8,128,128]{2,1,0:T(8,128)(2,1)S(1)} %get-tuple-element.65), channel_id=1, source_target_pairs={{0,1},{1,0},{2,3},{3,2},{4,5},{5,4},{6,7},{7,6},{8,9},{9,8},{10,11... | collective-permute-start | bytes 786440 | tf_op jit(solution)/shard_map/ppermute | solution.py:38
Sparse Core Ops, SparseCore 0:
  9.8 102.4 all-gather.4
where the time goes:
time: 178 us; the launch traced here: 177 us
  waiting for transfers between devices  70.3 us (39%)
  starting transfers between devices  48.7 us (27%)
  Pallas kernels  24.2 us (14%)
  between operations  14.8 us (8%)
  local copies, waits for them, and re-layouts  12.5 us (7%)
  other arithmetic  6.14 us (3%)
    ppermute x24, waiting for transfers between devices, shift_side(): return lax.ppermute(array, ('row', 'depth'), side_ring(shift, second))  55.5 us
    ppermute x24, starting transfers between devices, shift_side(): return lax.ppermute(array, ('row', 'depth'), side_ring(shift, second))  25.8 us
    all_to_all x1, starting transfers between devices, on_device(): lax.all_to_all(jnp.broadcast_to(overflow, (256, 1, 128)), AXES, 0, 0, til...  17.4 us
    pallas_call x1, Pallas kernels, sends(): pl.pallas_call(sends_kernel, out_shape=jax.ShapeDtypeStruct((32,), jnp.in...  9.22 us
    all_gather x1, waiting for transfers between devices, on_device(): ham = lax.all_gather(ham_pair, ('col', 'depth'), axis=0, tiled=True)  8.61 us
    pallas_call x2, Pallas kernels, combine(): pl.pallas_call(functools.partial(combine_kernel, len(panels)), out_shape=...  7.05 us
    ppermute x3, starting transfers between devices, swap(): return lax.ppermute(array, 'depth', [(0, 1), (1, 0)])  5.46 us
    all_to_all x1, waiting for transfers between devices, on_device(): lax.all_to_all(jnp.broadcast_to(overflow, (256, 1, 128)), AXES, 0, 0, til...  5.14 us
  transfers between devices with their start and end apart: 29, of which 15 were waited for; matrix products, arithmetic and copies ran while one was open for 4% of the time, Pallas kernels for 8%

commit v1 on v0

--- a/solution.py
+++ b/solution.py
@@ -10,6 +10,7 @@
 ROWS, COLS, CORES = 16, 8, 2
 SIDE = 4
 CAP = 8
+VMEM_BYTES = 56 * 1024 * 1024
 AXES = ("row", "col", "depth")
 HBM = pl.BlockSpec(memory_space=pltpu.HBM)
 VMEM = pl.BlockSpec(memory_space=pltpu.VMEM)
@@ -38,9 +39,9 @@
     return lax.ppermute(array, "depth", [(0, 1), (1, 0)])
 
 
-def combine_kernel(n_panels, table, ham, *refs):
-    panels = refs[:n_panels]
-    cheb_old, tang_old, cheb_new, tang_new, ham_buf, panel_buf, acc, sems = refs[n_panels:]
+def combine_kernel(n_panels, apart, table, ham, *refs):
+    panels, old, new = refs[:n_panels], refs[n_panels], refs[n_panels + 1 : -4]
+    ham_buf, panel_buf, acc, sems = refs[-4:]
 
     def issue(entry, carry):
         chunk, i = lax.shift_right_logical(entry, 2), entry & 3
@@ -80,28 +81,32 @@
 
     for out in range(8):
         scale = table[KEEP_AT + out].astype(jnp.float32)
-        old = cheb_old[out].astype(jnp.float32)
-        cheb_new[out] = (scale * (2.0 * acc[out, :, :128] - old)).astype(jnp.bfloat16)
-        old = tang_old[out].astype(jnp.float32)
-        tang_new[out] = (scale * (2.0 * acc[out, :, 128:] - old)).astype(jnp.bfloat16)
-
-
-def combine(table, ham, panels, cheb_old, tang_old):
-    shape = jax.ShapeDtypeStruct(cheb_old.shape, jnp.bfloat16)
+        for kind in range(2):
+            total = acc[out, :, 128 * kind : 128 * (kind + 1)]
+            value = scale * (2.0 * total - old[out, kind].astype(jnp.float32))
+            if apart:
+                new[kind][out] = value.astype(jnp.bfloat16)
+            else:
+                new[0][out, kind] = value.astype(jnp.bfloat16)
+
+
+def combine(table, ham, panels, old, apart):
+    one = jax.ShapeDtypeStruct((8, 128, 128), jnp.bfloat16)
+    both = jax.ShapeDtypeStruct(old.shape, jnp.bfloat16)
     return pl.pallas_call(
-        functools.partial(combine_kernel, len(panels)),
-        out_shape=(shape, shape),
-        in_specs=[SMEM, HBM] + [ANY] * len(panels) + [VMEM] * 2,
-        out_specs=(VMEM, VMEM),
+        functools.partial(combine_kernel, len(panels), apart),
+        out_shape=(one, one) if apart else both,
+        in_specs=[SMEM, HBM] + [HBM] * len(panels) + [VMEM],
+        out_specs=(VMEM, VMEM) if apart else VMEM,
         scratch_shapes=[
             pltpu.VMEM((16, 4, 2, 128, 128), jnp.bfloat16),
             pltpu.VMEM((16, 4, 2, 128, 128), jnp.bfloat16),
             pltpu.VMEM((9, 128, 256), jnp.float32),
             pltpu.SemaphoreType.DMA((2, 16)),
         ],
-        compiler_params=pltpu.CompilerParams(vmem_limit_bytes=24 * 1024 * 1024),
+        compiler_params=pltpu.CompilerParams(vmem_limit_bytes=VMEM_BYTES),
         cost_estimate=pl.CostEstimate(flops=1 << 30, bytes_accessed=1 << 23, transcendentals=0),
-    )(table, ham, *panels, cheb_old, tang_old)
+    )(table, ham, *panels, old)
 
 
 def pack_kernel(table, *refs):
@@ -138,6 +143,7 @@
         in_specs=[SMEM] + [ANY] * SIDE,
         out_specs=(VMEM,) * 3,
         scratch_shapes=[pltpu.SemaphoreType.DMA((3 * CAP,))],
+        compiler_params=pltpu.CompilerParams(vmem_limit_bytes=VMEM_BYTES),
         cost_estimate=pl.CostEstimate(flops=0, bytes_accessed=1 << 22, transcendentals=0),
     )(table, *panels)
 
@@ -289,13 +295,9 @@
     def mine(array):
         return lax.dynamic_slice_in_dim(array, 2 * layer, 2, 0)
 
-    def own(array):
-        return mine(array).reshape(8, 128, 128)
-
     def paired(cheb, tang):
-        return jnp.stack([cheb, tang], axis=1)
-
-    cheb, tang = own(cheb_cur), own(tang_cur)
+        return jnp.stack([mine(cheb).reshape(8, 128, 128), mine(tang).reshape(8, 128, 128)], axis=1)
+
     ham_pair = jnp.stack([ham_blocks[:, 0], deriv_blocks[:, 0]], axis=1)
     ham = lax.all_gather(ham_pair, ("col", "depth"), axis=0, tiled=True)
 
@@ -317,27 +319,28 @@
         across += [shift_side(piece, 1, True) for piece in before[2:]]
         return here + after + across + before, ready
 
-    def sparse_step(ham, cheb, tang, cheb_old, tang_old):
-        near_pieces = nearby(paired(cheb, tang))
+    def sparse_step(ham, now, old):
+        near_pieces = nearby(now)
         packed = pack(pack_table, near_pieces)
         arrived = [shift_side(packed[b - 1], b, True) for b in (1, 2, 3)]
-        return combine(sparse_table, ham, near_pieces + arrived, cheb_old, tang_old)
-
-    def dense_step(ham, cheb, tang, cheb_old, tang_old):
-        panel = lax.all_gather(paired(cheb, tang), "row", axis=0, tiled=True)
-        return combine(dense_table, ham, [panel], cheb_old, tang_old)
-
-    panel, (flags, pack_table) = ring_panel(paired(cheb, tang), (flags, pack_table))
+        return combine(sparse_table, ham, near_pieces + arrived, old, True)
+
+    def dense_step(ham, now, old):
+        panel = lax.all_gather(now, "row", axis=0, tiled=True)
+        return combine(dense_table, ham, [panel], old, True)
+
+    now = paired(cheb_cur, tang_cur)
+    panel, (flags, pack_table) = ring_panel(now, (flags, pack_table))
     crowded = jnp.max(flags) > 0
-    cheb_mid, tang_mid = combine(ring_table, ham, panel, own(cheb_prev), own(tang_prev))
-    cheb_new, tang_new = lax.cond(crowded, dense_step, sparse_step, ham, cheb_mid, tang_mid, cheb, tang)
-
-    def whole(array):
-        other = swap(array)
-        both = jnp.stack([jnp.where(layer == 0, array, other), jnp.where(layer == 0, other, array)])
+    middle = combine(ring_table, ham, panel, paired(cheb_prev, tang_prev), False)
+    last = lax.cond(crowded, dense_step, sparse_step, ham, middle, now)
+
+    def whole(mine):
+        theirs = swap(mine)
+        both = jnp.stack([jnp.where(layer == 0, mine, theirs), jnp.where(layer == 0, theirs, mine)])
         return both.reshape(4, 4, 128, 128)
 
-    return whole(cheb_new), whole(tang_new)
+    return whole(last[0]), whole(last[1])
 
 
 def solution(mesh):

time: 178 us -> 170 us (0.955)
  local copies, waits for them, and re-layouts: 12.5 us -> 6.63 us
    cond x16 -> x12, local copies, waits for them, and re-layouts: 4.98 us -> 1.6 us
    unnamed x19 -> x21, local copies, waits for them, and re-layouts: 3.24 us -> 0.8 us
  transfers between devices with their start and end apart: 29 -> 29, of which waited for: 15 -> 16; matrix products, arithmetic and copies ran while one was open for 4% -> 5% of each run, Pallas kernels for 8% -> 8%
where the time goes in v1:
time: 170 us; the launch traced here: 169 us
  waiting for transfers between devices  69.4 us (41%)
  starting transfers between devices  49.2 us (29%)
  Pallas kernels  23.3 us (14%)
  between operations  14.8 us (9%)
  local copies, waits for them, and re-layouts  6.63 us (4%)
  other arithmetic  5.99 us (4%)
    ppermute x24, waiting for transfers between devices, shift_side(): return lax.ppermute(array, ('row', 'depth'), side_ring(shift, second))  53.7 us
    ppermute x24, starting transfers between devices, shift_side(): return lax.ppermute(array, ('row', 'depth'), side_ring(shift, second))  26 us
    all_to_all x1, starting transfers between devices, on_device(): lax.all_to_all(jnp.broadcast_to(overflow, (256, 1, 128)), AXES, 0, 0, til...  17.4 us
    all_gather x1, waiting for transfers between devices, on_device(): ham = lax.all_gather(ham_pair, ('col', 'depth'), axis=0, tiled=True)  9.44 us
    pallas_call x1, Pallas kernels, sends(): pl.pallas_call(sends_kernel, out_shape=jax.ShapeDtypeStruct((32,), jnp.in...  9.22 us
    pallas_call x2, Pallas kernels, combine(): pl.pallas_call(functools.partial(combine_kernel, len(panels), apart), out...  6.18 us
    ppermute x3, starting transfers between devices, swap(): return lax.ppermute(array, 'depth', [(0, 1), (1, 0)])  5.78 us
    all_to_all x1, waiting for transfers between devices, on_device(): lax.all_to_all(jnp.broadcast_to(overflow, (256, 1, 128)), AXES, 0, 0, til...  5.16 us
  transfers between devices with their start and end apart: 29, of which 16 were waited for; matrix products, arithmetic and copies ran while one was open for 5% of the time, Pallas kernels for 8%

profile of v1, /device:TPU:1, one launch (start us, length us, event | category | flops | bytes accessed | tf_op | source)
XLA Modules:
  0.0 169.4 jit_solution(8261217981067759047)
XLA Ops:
  7.2 2.3 %pad_maximum_fusion = bf16[16,2,128,128]{3,2,1,0:T(8,128)(2,1)} fusion(bf16[16,1,128,128]{3,2,1,0:T(8,128)(2,1)} %param.12, bf16[16,1,128,128]{3,2,1,0:T(8,128)(2,1)} %param.11), kind=kLoop, calls=%fused_computation | loop fusion | flops 524288 | bytes 2097152 | tf_op jit(solution)/shard_map/stack | solution.py:301
  9.6 0.8 copy.22.cols
  10.3 3.2 %collective-permute-start.7 = (s32[16,8]{1,0:T(8,128)S(1)}, s32[16,8]{1,0:T(8,128)S(1)}, u32[]{:S(2)}, u32[]{:S(2)}) collective-permute-start(s32[16,8]{1,0:T(8,128)S(1)} %copy.22.cols), channel_id=1, source_target_pairs={{0,1},{1,0},{2,3},{3,2},{4,5},{5,4},{6,7},{7,6},{8,9},{9,8},{10,11... | collective-permute-start | bytes 1544 | tf_op jit(solution)/shard_map/ppermute | solution.py:39
  13.6 1.1 constant_dynamic-slice_fusion.2
  14.6 0.8 reshape.14
  15.4 0.8 collective-permute-start.8
  17.4 2.8 %collective-permute-start.11 = (bf16[8,2,128,128]{3,2,1,0:T(8,128)(2,1)S(1)}, bf16[8,2,128,128]{3,2,1,0:T(8,128)(2,1)S(1)}, u32[]{:S(2)}, u32[]{:S(2)}) collective-permute-start(bf16[8,2,128,128]{3,2,1,0:T(8,128)(2,1)S(1)} %pad_maximum_fusion.1.refs_0_), channel_id=1, source_target_pairs={{0,48},{1,193},{16,0},{17,209},{32,16},{33,225},{48,32},{49,241},{... | collective-permute-start | bytes 1572872 | tf_op jit(solution)/shard_map/ppermute | solution.py:35
  20.6 0.7 collective-permute-start.13
  21.3 2.1 %collective-permute-start.6 = (bf16[8,2,128,128]{3,2,1,0:T(8,128)(2,1)S(1)}, bf16[8,2,128,128]{3,2,1,0:T(8,128)(2,1)S(1)}, u32[]{:S(2)}, u32[]{:S(2)}) collective-permute-start(bf16[8,2,128,128]{3,2,1,0:T(8,128)(2,1)S(1)} %pad_maximum_fusion.1.refs_0_), channel_id=1, source_target_pairs={{0,192},{1,49},{16,208},{17,1},{32,224},{33,17},{48,240},{49,33},{... | collective-permute-start | bytes 1572872 | tf_op jit(solution)/shard_map/ppermute | solution.py:35
  23.4 6.6 %collective-permute-done.11.refs_1_ = bf16[8,2,128,128]{3,2,1,0:T(8,128)(2,1)S(1)} collective-permute-done((bf16[8,2,128,128]{3,2,1,0:T(8,128)(2,1)S(1)}, bf16[8,2,128,128]{3,2,1,0:T(8,128)(2,1)S(1)}, u32[]{:S(2)}, u32[]{:S(2)}) %collective-permute-start.11) | collective-permute-done | bytes 524320 | tf_op jit(solution)/shard_map/ppermute | solution.py:35
  30.0 2.1 %collective-permute-start.14 = (bf16[8,2,128,128]{3,2,1,0:T(8,128)(2,1)S(1)}, bf16[8,2,128,128]{3,2,1,0:T(8,128)(2,1)}, u32[]{:S(2)}, u32[]{:S(2)}) collective-permute-start(bf16[8,2,128,128]{3,2,1,0:T(8,128)(2,1)S(1)} %collective-permute-done.11.refs_1_), channel_id=1, source_target_pairs={{0,192},{1,49},{16,208},{17,1},{32,224},{33,17},{48,240},{49,33},{... | collective-permute-start | bytes 1572872 | tf_op jit(solution)/shard_map/ppermute | solution.py:35
  32.1 2.0 %collective-permute-start.15 = (bf16[8,2,128,128]{3,2,1,0:T(8,128)(2,1)S(1)}, bf16[8,2,128,128]{3,2,1,0:T(8,128)(2,1)}, u32[]{:S(2)}, u32[]{:S(2)}) collective-permute-start(bf16[8,2,128,128]{3,2,1,0:T(8,128)(2,1)S(1)} %collective-permute-done.12.refs_2_), channel_id=1, source_target_pairs={{0,192},{1,49},{16,208},{17,1},{32,224},{33,17},{48,240},{49,33},{... | collective-permute-start | bytes 1572872 | tf_op jit(solution)/shard_map/ppermute | solution.py:35
  34.1 6.4 %collective-permute-done.13.refs_3_ = bf16[8,2,128,128]{3,2,1,0:T(8,128)(2,1)S(1)} collective-permute-done((bf16[8,2,128,128]{3,2,1,0:T(8,128)(2,1)S(1)}, bf16[8,2,128,128]{3,2,1,0:T(8,128)(2,1)S(1)}, u32[]{:S(2)}, u32[]{:S(2)}) %collective-permute-start.13) | collective-permute-done | bytes 524320 | tf_op jit(solution)/shard_map/ppermute | solution.py:35
  40.5 2.1 %collective-permute-start.16 = (bf16[8,2,128,128]{3,2,1,0:T(8,128)(2,1)S(1)}, bf16[8,2,128,128]{3,2,1,0:T(8,128)(2,1)}, u32[]{:S(2)}, u32[]{:S(2)}) collective-permute-start(bf16[8,2,128,128]{3,2,1,0:T(8,128)(2,1)S(1)} %collective-permute-done.13.refs_3_), channel_id=1, source_target_pairs={{0,192},{1,49},{16,208},{17,1},{32,224},{33,17},{48,240},{49,33},{... | collective-permute-start | bytes 1572872 | tf_op jit(solution)/shard_map/ppermute | solution.py:35
  43.6 4.9 %shard_map.104 = (s32[208]{0:T(256)}, s32[208]{0:T(256)S(1)}, s32[208]{0:T(256)S(1)}, s32[1]{0:T(128)}) custom-call(s32[4,64]{1,0:T(4,128)} %rows.3, s32[16,8]{1,0:T(8,128)} %copy-done.12, s32[16,8]{1,0:T(8,128)} %copy-done.13, s32[4,4]{1,0:T(4,128)} %keep.1), custom_call_target="tpu_custom_call" | custom-call | tf_op jit(solution)/shard_map/pallas_call | solution.py:229
  48.5 1.3 broadcast_in_dim.2
  49.8 17.4 %all-to-all-start = ((s32[256,1,128]{2,1,0:T(1,128)}), s32[256,1,128]{2,1,0:T(1,128)S(1)}, u32[]{:S(2)}, u32[]{:S(2)}) async-start(s32[256,1,128]{2,1,0:T(1,128)} %broadcast_in_dim.2), calls=%async_computation | async-start | bytes 262144 | tf_op jit(solution)/shard_map/all_to_all | solution.py:306
  67.3 9.2 %shard_map.105 = s32[32]{0:T(128)S(1)} custom-call(s32[4,64]{1,0:T(4,128)} %rows.3, s32[34,8]{1,0:T(8,128)} %copy-done.14, s32[34,8]{1,0:T(8,128)} %copy-done.15, s32[34,8]{1,0:T(8,128)} %copy-done.16), custom_call_target="tpu_custom_call" | custom-call | tf_op jit(solution)/shard_map/pallas_call | solution.py:273
  76.5 5.2 %all-to-all-done = s32[256,1,128]{2,1,0:T(1,128)S(1)} async-done(((s32[256,1,128]{2,1,0:T(1,128)}), s32[256,1,128]{2,1,0:T(1,128)S(1)}, u32[]{:S(2)}, u32[]{:S(2)}) %all-to-all-start) | async-done | bytes 131104 | tf_op jit(solution)/shard_map/all_to_all | solution.py:306
  82.0 1.2 collective-permute-start.24
  83.2 1.5 collective-permute-start.18
  84.8 1.1 constant_dynamic-slice_fusion
  85.8 0.9 pad_maximum_fusion.2.refs_16_
  86.8 0.9 reduce_max.9
  88.3 1.8 %collective-permute-done.17.refs_8_ = bf16[8,2,128,128]{3,2,1,0:T(8,128)(2,1)} collective-permute-done((bf16[8,2,128,128]{3,2,1,0:T(8,128)(2,1)S(1)}, bf16[8,2,128,128]{3,2,1,0:T(8,128)(2,1)}, u32[]{:S(2)}, u32[]{:S(2)}) %collective-permute-start.17) | collective-permute-done | bytes 524320 | tf_op jit(solution)/shard_map/ppermute | solution.py:35
  90.1 1.5 collective-permute-done.24.refs_13_
  91.6 4.1 %collective-permute-done.18.refs_9_ = bf16[8,2,128,128]{3,2,1,0:T(8,128)(2,1)} collective-permute-done((bf16[8,2,128,128]{3,2,1,0:T(8,128)(2,1)}, bf16[8,2,128,128]{3,2,1,0:T(8,128)(2,1)}, u32[]{:S(2)}, u32[]{:S(2)}) %collective-permute-start.18) | collective-permute-done | bytes 524320 | tf_op jit(solution)/shard_map/ppermute | solution.py:35
  95.7 1.5 collective-permute-done.20.refs_10_
  97.2 5.6 %collective-permute-done.22.refs_11_ = bf16[8,2,128,128]{3,2,1,0:T(8,128)(2,1)} collective-permute-done((bf16[8,2,128,128]{3,2,1,0:T(8,128)(2,1)}, bf16[8,2,128,128]{3,2,1,0:T(8,128)(2,1)}, u32[]{:S(2)}, u32[]{:S(2)}) %collective-permute-start.22) | collective-permute-done | bytes 524320 | tf_op jit(solution)/shard_map/ppermute | solution.py:35
  102.9 9.4 %all-gather.5.cloned.1.call-done.ham = bf16[256,2,128,128]{3,2,1,0:T(8,128)(2,1)} async-done(((bf16[16,2,128,128]{3,2,1,0:T(8,128)(2,1)}), bf16[256,2,128,128]{3,2,1,0:T(8,128)(2,1)}) %all-gather.5.cloned.1.call-update) | async-done | bytes 16777232 | tf_op jit(solution)/shard_map/all_gather | solution.py:302
  112.3 3.3 %shard_map.106 = bf16[8,2,128,128]{3,2,1,0:T(8,128)(2,1)S(1)} custom-call(s32[208]{0:T(256)} %get-tuple-element.43.table, bf16[256,2,128,128]{3,2,1,0:T(8,128)(2,1)} %all-gather.5.cloned.1.call-done.ham, bf16[8,2,128,128]{3,2,1,0:T(8,128)(2,1)S(1)} %pad_maximum_fusion.1.refs_0_, bf16[8,2,128,128]{3,2,1,0:T(8,128)(2,1)} %copy-done.4, ...), custom_call_target="tpu_custom_call" | custom-call | flops 1073741824 | bytes 8388608 | tf_op jit(solution)/shard_map/pallas_call | solution.py:96
  115.7 41.5 %conditional.1 = ((bf16[8,128,128]{2,1,0:T(8,128)(2,1)S(1)}, bf16[8,128,128]{2,1,0:T(8,128)(2,1)S(1)})) conditional(s32[]{:T(128)} %convert_element_type.3, (bf16[8,2,128,128]{3,2,1,0:T(8,128)(2,1)S(1)}, s32[32]{0:T(128)S(1)}, s32[208]{0:T(256)S(1)}, bf16[256,2,128,128]{3,2,1,0:T(8,128)(2,1)}, bf16[8,2,128,128]{3,2,1,0:T(8,128)(2,1)S(1)}) %tuple.16, ...), branch_computations={%region_1.0_spmd, %region_2.0_spmd} | conditional | flops 1073741824 | bytes 37749152 | solution.py:336
  115.7 2.5 %collective-permute-start = (bf16[8,2,128,128]{3,2,1,0:T(8,128)(2,1)S(1)}, bf16[8,2,128,128]{3,2,1,0:T(8,128)(2,1)S(1)}, u32[]{:S(2)}, u32[]{:S(2)}) collective-permute-start(bf16[8,2,128,128]{3,2,1,0:T(8,128)(2,1)S(1)} %get-tuple-element.20.refs_0_), channel_id=1, source_target_pairs={{0,48},{1,193},{16,0},{17,209},{32,16},{33,225},{48,32},{49,241},{... | collective-permute-start | bytes 1572872 | tf_op jit(solution)/shard_map/cond/branch_0_fun/ppermute | solution.py:35
  118.9 0.8 collective-permute-start.2
  119.6 10.4 %collective-permute-done.refs_1_ = bf16[8,2,128,128]{3,2,1,0:T(8,128)(2,1)S(1)} collective-permute-done((bf16[8,2,128,128]{3,2,1,0:T(8,128)(2,1)S(1)}, bf16[8,2,128,128]{3,2,1,0:T(8,128)(2,1)S(1)}, u32[]{:S(2)}, u32[]{:S(2)}) %collective-permute-start) | collective-permute-done | bytes 524320 | tf_op jit(solution)/shard_map/cond/branch_0_fun/ppermute | solution.py:35
  130.0 3.7 %collective-permute-done.2.refs_3_ = bf16[8,2,128,128]{3,2,1,0:T(8,128)(2,1)S(1)} collective-permute-done((bf16[8,2,128,128]{3,2,1,0:T(8,128)(2,1)S(1)}, bf16[8,2,128,128]{3,2,1,0:T(8,128)(2,1)S(1)}, u32[]{:S(2)}, u32[]{:S(2)}) %collective-permute-start.2) | collective-permute-done | bytes 524320 | tf_op jit(solution)/shard_map/cond/branch_0_fun/ppermute | solution.py:35
  133.7 0.8 copy-done.3
  134.5 3.0 %branch_0_fun.2 = (bf16[8,2,128,128]{3,2,1,0:T(8,128)(2,1)}, bf16[8,2,128,128]{3,2,1,0:T(8,128)(2,1)}, bf16[8,2,128,128]{3,2,1,0:T(8,128)(2,1)}) custom-call(s32[32]{0:T(128)S(1)} %get-tuple-element.21.table, bf16[8,2,128,128]{3,2,1,0:T(8,128)(2,1)S(1)} %get-tuple-element.20.refs_0_, bf16[8,2,128,128]{3,2,1,0:T(8,128)(2,1)} %copy-done.1, ...), custom_call_target="tpu_custom_call" | custom-call | bytes 4194304 | tf_op jit(solution)/shard_map/cond/branch_0_fun/pallas_call | solution.py:140
  137.5 0.7 collective-permute-start.3
  138.2 2.3 %collective-permute-start.4 = (bf16[8,2,128,128]{3,2,1,0:T(8,128)(2,1)}, bf16[8,2,128,128]{3,2,1,0:T(8,128)(2,1)S(1)}, u32[]{:S(2)}, u32[]{:S(2)}) collective-permute-start(bf16[8,2,128,128]{3,2,1,0:T(8,128)(2,1)} %get-tuple-element.23), channel_id=1, source_target_pairs={{0,128},{1,33},{16,144},{17,49},{32,160},{33,1},{48,176},{49,17},{... | collective-permute-start | bytes 1572872 | tf_op jit(solution)/shard_map/cond/branch_0_fun/ppermute | solution.py:35
  140.5 1.5 collective-permute-start.5
  142.0 5.3 %collective-permute-done.3.refs_4_ = bf16[8,2,128,128]{3,2,1,0:T(8,128)(2,1)S(1)} collective-permute-done((bf16[8,2,128,128]{3,2,1,0:T(8,128)(2,1)}, bf16[8,2,128,128]{3,2,1,0:T(8,128)(2,1)S(1)}, u32[]{:S(2)}, u32[]{:S(2)}) %collective-permute-start.3) | collective-permute-done | bytes 524320 | tf_op jit(solution)/shard_map/cond/branch_0_fun/ppermute | solution.py:35
  147.3 5.9 %collective-permute-done.4.refs_5_ = bf16[8,2,128,128]{3,2,1,0:T(8,128)(2,1)S(1)} collective-permute-done((bf16[8,2,128,128]{3,2,1,0:T(8,128)(2,1)}, bf16[8,2,128,128]{3,2,1,0:T(8,128)(2,1)S(1)}, u32[]{:S(2)}, u32[]{:S(2)}) %collective-permute-start.4) | collective-permute-done | bytes 524320 | tf_op jit(solution)/shard_map/cond/branch_0_fun/ppermute | solution.py:35
  154.3 2.8 %branch_0_fun.3 = (bf16[8,128,128]{2,1,0:T(8,128)(2,1)S(1)}, bf16[8,128,128]{2,1,0:T(8,128)(2,1)S(1)}) custom-call(s32[208]{0:T(256)S(1)} %get-tuple-element.18.table, bf16[256,2,128,128]{3,2,1,0:T(8,128)(2,1)} %get-tuple-element.19.ham, bf16[8,2,128,128]{3,2,1,0:T(8,128)(2,1)S(1)} %get-tuple-element.20.refs_0_, bf16[8,2,128,128]{3,2,1,0:T(8,128)(2,1)} %copy-done.1, ...), custom_call_target="tpu_custom_call" | custom-call | flops 1073741824 | bytes 8388608 | tf_op jit(solution)/shard_map/cond/branch_0_fun/pallas_call | solution.py:96
  157.2 2.4 %collective-permute-start.25 = (bf16[8,128,128]{2,1,0:T(8,128)(2,1)S(1)}, bf16[8,128,128]{2,1,0:T(8,128)(2,1)S(1)}, u32[]{:S(2)}, u32[]{:S(2)}) collective-permute-start(bf16[8,128,128]{2,1,0:T(8,128)(2,1)S(1)} %get-tuple-element.48), channel_id=1, source_target_pairs={{0,1},{1,0},{2,3},{3,2},{4,5},{5,4},{6,7},{7,6},{8,9},{9,8},{10,11... | collective-permute-start | bytes 786440 | tf_op jit(solution)/shard_map/ppermute | solution.py:39
  159.7 1.1 collective-permute-done.25
  160.8 0.8 pad_maximum_fusion.3
  161.7 0.8 pad_maximum_fusion.4
  (63 shorter events, 4.9 us)
Async XLA Ops:
  7.2 105.1 %all-gather.5.cloned.1.call-start = ((), (), s32[]{:S(2)}) async-start(), calls=%async_computation.2 | async-start | bytes 17825792 | tf_op jit(solution)/shard_map/all_gather | solution.py:302
  10.3 33.2 %copy-start.12 = (s32[16,8]{1,0:T(8,128)}, s32[16,8]{1,0:T(8,128)S(1)}, u32[]{:S(2)}) copy-start(s32[16,8]{1,0:T(8,128)S(1)} %copy.22.cols) | copy-start | bytes 1540
  10.3 5.1 %collective-permute-start.7 = (s32[16,8]{1,0:T(8,128)S(1)}, s32[16,8]{1,0:T(8,128)S(1)}, u32[]{:S(2)}, u32[]{:S(2)}) collective-permute-start(s32[16,8]{1,0:T(8,128)S(1)} %copy.22.cols), channel_id=1, source_target_pairs={{0,1},{1,0},{2,3},{3,2},{4,5},{5,4},{6,7},{7,6},{8,9},{9,8},{10,11... | collective-permute-start | bytes 1544 | tf_op jit(solution)/shard_map/ppermute | solution.py:39
  15.4 28.2 %copy-start.13 = (s32[16,8]{1,0:T(8,128)}, s32[16,8]{1,0:T(8,128)S(1)}, u32[]{:S(2)}) copy-start(s32[16,8]{1,0:T(8,128)S(1)} %collective-permute-done.7.other_cols) | copy-start | bytes 1540
  15.4 5.2 %collective-permute-start.8 = (s32[34,8]{1,0:T(8,128)S(1)}, s32[34,8]{1,0:T(8,128)S(1)}, u32[]{:S(2)}, u32[]{:S(2)}) collective-permute-start(s32[34,8]{1,0:T(8,128)S(1)} %pad_add_fusion), channel_id=1, source_target_pairs={{0,192},{1,49},{16,208},{17,1},{32,224},{33,17},{48,240},{49,33},{... | collective-permute-start | bytes 3272 | tf_op jit(solution)/shard_map/ppermute | solution.py:35
  16.2 5.0 %collective-permute-start.9 = (s32[34,8]{1,0:T(8,128)S(1)}, s32[34,8]{1,0:T(8,128)S(1)}, u32[]{:S(2)}, u32[]{:S(2)}) collective-permute-start(s32[34,8]{1,0:T(8,128)S(1)} %pad_add_fusion), channel_id=1, source_target_pairs={{0,128},{1,33},{16,144},{17,49},{32,160},{33,1},{48,176},{49,17},{... | collective-permute-start | bytes 3272 | tf_op jit(solution)/shard_map/ppermute | solution.py:35
  16.8 6.6 %collective-permute-start.10 = (s32[34,8]{1,0:T(8,128)S(1)}, s32[34,8]{1,0:T(8,128)S(1)}, u32[]{:S(2)}, u32[]{:S(2)}) collective-permute-start(s32[34,8]{1,0:T(8,128)S(1)} %pad_add_fusion), channel_id=1, source_target_pairs={{0,64},{1,17},{16,80},{17,33},{32,96},{33,49},{48,112},{49,1},{64,... | collective-permute-start | bytes 3272 | tf_op jit(solution)/shard_map/ppermute | solution.py:35
  17.4 12.6 %collective-permute-start.11 = (bf16[8,2,128,128]{3,2,1,0:T(8,128)(2,1)S(1)}, bf16[8,2,128,128]{3,2,1,0:T(8,128)(2,1)S(1)}, u32[]{:S(2)}, u32[]{:S(2)}) collective-permute-start(bf16[8,2,128,128]{3,2,1,0:T(8,128)(2,1)S(1)} %pad_maximum_fusion.1.refs_0_), channel_id=1, source_target_pairs={{0,48},{1,193},{16,0},{17,209},{32,16},{33,225},{48,32},{49,241},{... | collective-permute-start | bytes 1572872 | tf_op jit(solution)/shard_map/ppermute | solution.py:35
  20.2 11.9 %collective-permute-start.12 = (bf16[8,2,128,128]{3,2,1,0:T(8,128)(2,1)S(1)}, bf16[8,2,128,128]{3,2,1,0:T(8,128)(2,1)S(1)}, u32[]{:S(2)}, u32[]{:S(2)}) collective-permute-start(bf16[8,2,128,128]{3,2,1,0:T(8,128)(2,1)S(1)} %pad_maximum_fusion.1.refs_0_), channel_id=1, source_target_pairs={{0,32},{1,129},{16,48},{17,145},{32,0},{33,161},{48,16},{49,177},{... | collective-permute-start | bytes 1572872 | tf_op jit(solution)/shard_map/ppermute | solution.py:35
  20.6 46.7 %copy-start.14 = (s32[34,8]{1,0:T(8,128)}, s32[34,8]{1,0:T(8,128)S(1)}, u32[]{:S(2)}) copy-start(s32[34,8]{1,0:T(8,128)S(1)} %collective-permute-done.8.refs_0_) | copy-start | bytes 3268
  20.6 20.0 %collective-permute-start.13 = (bf16[8,2,128,128]{3,2,1,0:T(8,128)(2,1)S(1)}, bf16[8,2,128,128]{3,2,1,0:T(8,128)(2,1)S(1)}, u32[]{:S(2)}, u32[]{:S(2)}) collective-permute-start(bf16[8,2,128,128]{3,2,1,0:T(8,128)(2,1)S(1)} %pad_maximum_fusion.1.refs_0_), channel_id=1, source_target_pairs={{0,16},{1,65},{16,32},{17,81},{32,48},{33,97},{48,0},{49,113},{64,... | collective-permute-start | bytes 1572872 | tf_op jit(solution)/shard_map/ppermute | solution.py:35
  21.3 46.0 %copy-start.15 = (s32[34,8]{1,0:T(8,128)}, s32[34,8]{1,0:T(8,128)S(1)}, u32[]{:S(2)}) copy-start(s32[34,8]{1,0:T(8,128)S(1)} %collective-permute-done.9.refs_1_) | copy-start | bytes 3268
  21.3 21.3 %collective-permute-start.6 = (bf16[8,2,128,128]{3,2,1,0:T(8,128)(2,1)S(1)}, bf16[8,2,128,128]{3,2,1,0:T(8,128)(2,1)S(1)}, u32[]{:S(2)}, u32[]{:S(2)}) collective-permute-start(bf16[8,2,128,128]{3,2,1,0:T(8,128)(2,1)S(1)} %pad_maximum_fusion.1.refs_0_), channel_id=1, source_target_pairs={{0,192},{1,49},{16,208},{17,1},{32,224},{33,17},{48,240},{49,33},{... | collective-permute-start | bytes 1572872 | tf_op jit(solution)/shard_map/ppermute | solution.py:35
  23.4 43.9 %copy-start.16 = (s32[34,8]{1,0:T(8,128)}, s32[34,8]{1,0:T(8,128)S(1)}, u32[]{:S(2)}) copy-start(s32[34,8]{1,0:T(8,128)S(1)} %collective-permute-done.10.refs_2_) | copy-start | bytes 3268
  23.4 19.8 %collective-permute-start.23 = (bf16[8,2,128,128]{3,2,1,0:T(8,128)(2,1)S(1)}, bf16[8,2,128,128]{3,2,1,0:T(8,128)(2,1)S(1)}, u32[]{:S(2)}, u32[]{:S(2)}) collective-permute-start(bf16[8,2,128,128]{3,2,1,0:T(8,128)(2,1)S(1)} %pad_maximum_fusion.1.refs_0_), channel_id=1, source_target_pairs={{0,64},{1,17},{16,80},{17,33},{32,96},{33,49},{48,112},{49,1},{64,... | collective-permute-start | bytes 1572872 | tf_op jit(solution)/shard_map/ppermute | solution.py:35
  30.0 82.3 %copy-start.4 = (bf16[8,2,128,128]{3,2,1,0:T(8,128)(2,1)}, bf16[8,2,128,128]{3,2,1,0:T(8,128)(2,1)S(1)}, u32[]{:S(2)}) copy-start(bf16[8,2,128,128]{3,2,1,0:T(8,128)(2,1)S(1)} %collective-permute-done.11.refs_1_) | copy-start | bytes 1572868
  30.0 51.7 %collective-permute-start.14 = (bf16[8,2,128,128]{3,2,1,0:T(8,128)(2,1)S(1)}, bf16[8,2,128,128]{3,2,1,0:T(8,128)(2,1)}, u32[]{:S(2)}, u32[]{:S(2)}) collective-permute-start(bf16[8,2,128,128]{3,2,1,0:T(8,128)(2,1)S(1)} %collective-permute-done.11.refs_1_), channel_id=1, source_target_pairs={{0,192},{1,49},{16,208},{17,1},{32,224},{33,17},{48,240},{49,33},{... | collective-permute-start | bytes 1572872 | tf_op jit(solution)/shard_map/ppermute | solution.py:35
  32.1 80.2 %copy-start.5 = (bf16[8,2,128,128]{3,2,1,0:T(8,128)(2,1)}, bf16[8,2,128,128]{3,2,1,0:T(8,128)(2,1)S(1)}, u32[]{:S(2)}) copy-start(bf16[8,2,128,128]{3,2,1,0:T(8,128)(2,1)S(1)} %collective-permute-done.12.refs_2_) | copy-start | bytes 1572868
  32.1 49.9 %collective-permute-start.15 = (bf16[8,2,128,128]{3,2,1,0:T(8,128)(2,1)S(1)}, bf16[8,2,128,128]{3,2,1,0:T(8,128)(2,1)}, u32[]{:S(2)}, u32[]{:S(2)}) collective-permute-start(bf16[8,2,128,128]{3,2,1,0:T(8,128)(2,1)S(1)} %collective-permute-done.12.refs_2_), channel_id=1, source_target_pairs={{0,192},{1,49},{16,208},{17,1},{32,224},{33,17},{48,240},{49,33},{... | collective-permute-start | bytes 1572872 | tf_op jit(solution)/shard_map/ppermute | solution.py:35
  40.5 71.8 %copy-start.6 = (bf16[8,2,128,128]{3,2,1,0:T(8,128)(2,1)}, bf16[8,2,128,128]{3,2,1,0:T(8,128)(2,1)S(1)}, u32[]{:S(2)}) copy-start(bf16[8,2,128,128]{3,2,1,0:T(8,128)(2,1)S(1)} %collective-permute-done.13.refs_3_) | copy-start | bytes 1572868
  40.5 42.6 %collective-permute-start.16 = (bf16[8,2,128,128]{3,2,1,0:T(8,128)(2,1)S(1)}, bf16[8,2,128,128]{3,2,1,0:T(8,128)(2,1)}, u32[]{:S(2)}, u32[]{:S(2)}) collective-permute-start(bf16[8,2,128,128]{3,2,1,0:T(8,128)(2,1)S(1)} %collective-permute-done.13.refs_3_), channel_id=1, source_target_pairs={{0,192},{1,49},{16,208},{17,1},{32,224},{33,17},{48,240},{49,33},{... | collective-permute-start | bytes 1572872 | tf_op jit(solution)/shard_map/ppermute | solution.py:35
  42.6 69.7 %copy-start.7 = (bf16[8,2,128,128]{3,2,1,0:T(8,128)(2,1)}, bf16[8,2,128,128]{3,2,1,0:T(8,128)(2,1)S(1)}, u32[]{:S(2)}) copy-start(bf16[8,2,128,128]{3,2,1,0:T(8,128)(2,1)S(1)} %collective-permute-done.6.refs_4_) | copy-start | bytes 1572868
  42.6 42.0 %collective-permute-start.19 = (bf16[8,2,128,128]{3,2,1,0:T(8,128)(2,1)S(1)}, bf16[8,2,128,128]{3,2,1,0:T(8,128)(2,1)}, u32[]{:S(2)}, u32[]{:S(2)}) collective-permute-start(bf16[8,2,128,128]{3,2,1,0:T(8,128)(2,1)S(1)} %collective-permute-done.12.refs_2_), channel_id=1, source_target_pairs={{0,64},{1,17},{16,80},{17,33},{32,96},{33,49},{48,112},{49,1},{64,... | collective-permute-start | bytes 1572872 | tf_op jit(solution)/shard_map/ppermute | solution.py:35
  43.1 69.2 %copy-start.8 = (bf16[8,2,128,128]{3,2,1,0:T(8,128)(2,1)}, bf16[8,2,128,128]{3,2,1,0:T(8,128)(2,1)S(1)}, u32[]{:S(2)}) copy-start(bf16[8,2,128,128]{3,2,1,0:T(8,128)(2,1)S(1)} %collective-permute-done.23.refs_12_) | copy-start | bytes 1572868
  43.2 41.5 %collective-permute-start.21 = (bf16[8,2,128,128]{3,2,1,0:T(8,128)(2,1)S(1)}, bf16[8,2,128,128]{3,2,1,0:T(8,128)(2,1)}, u32[]{:S(2)}, u32[]{:S(2)}) collective-permute-start(bf16[8,2,128,128]{3,2,1,0:T(8,128)(2,1)S(1)} %collective-permute-done.13.refs_3_), channel_id=1, source_target_pairs={{0,64},{1,17},{16,80},{17,33},{32,96},{33,49},{48,112},{49,1},{64,... | collective-permute-start | bytes 1572872 | tf_op jit(solution)/shard_map/ppermute | solution.py:35
  49.8 31.9 %all-to-all-start = ((s32[256,1,128]{2,1,0:T(1,128)}), s32[256,1,128]{2,1,0:T(1,128)S(1)}, u32[]{:S(2)}, u32[]{:S(2)}) async-start(s32[256,1,128]{2,1,0:T(1,128)} %broadcast_in_dim.2), calls=%async_computation | async-start | bytes 262144 | tf_op jit(solution)/shard_map/all_to_all | solution.py:306
  81.7 8.4 %collective-permute-start.17 = (bf16[8,2,128,128]{3,2,1,0:T(8,128)(2,1)S(1)}, bf16[8,2,128,128]{3,2,1,0:T(8,128)(2,1)}, u32[]{:S(2)}, u32[]{:S(2)}) collective-permute-start(bf16[8,2,128,128]{3,2,1,0:T(8,128)(2,1)S(1)} %collective-permute-done.6.refs_4_), channel_id=1, source_target_pairs={{0,192},{1,49},{16,208},{17,1},{32,224},{33,17},{48,240},{49,33},{... | collective-permute-start | bytes 1572872 | tf_op jit(solution)/shard_map/ppermute | solution.py:35
  82.0 9.6 %collective-permute-start.24 = (bf16[8,2,128,128]{3,2,1,0:T(8,128)(2,1)S(1)}, bf16[8,2,128,128]{3,2,1,0:T(8,128)(2,1)}, u32[]{:S(2)}, u32[]{:S(2)}) collective-permute-start(bf16[8,2,128,128]{3,2,1,0:T(8,128)(2,1)S(1)} %collective-permute-done.11.refs_1_), channel_id=1, source_target_pairs={{0,64},{1,17},{16,80},{17,33},{32,96},{33,49},{48,112},{49,1},{64,... | collective-permute-start | bytes 1572872 | tf_op jit(solution)/shard_map/ppermute | solution.py:35
  83.2 12.6 %collective-permute-start.18 = (bf16[8,2,128,128]{3,2,1,0:T(8,128)(2,1)}, bf16[8,2,128,128]{3,2,1,0:T(8,128)(2,1)}, u32[]{:S(2)}, u32[]{:S(2)}) collective-permute-start(bf16[8,2,128,128]{3,2,1,0:T(8,128)(2,1)} %collective-permute-done.14.refs_5_), channel_id=1, source_target_pairs={{0,192},{1,49},{16,208},{17,1},{32,224},{33,17},{48,240},{49,33},{... | collective-permute-start | bytes 1572872 | tf_op jit(solution)/shard_map/ppermute | solution.py:35
  84.7 12.6 %collective-permute-start.20 = (bf16[8,2,128,128]{3,2,1,0:T(8,128)(2,1)}, bf16[8,2,128,128]{3,2,1,0:T(8,128)(2,1)}, u32[]{:S(2)}, u32[]{:S(2)}) collective-permute-start(bf16[8,2,128,128]{3,2,1,0:T(8,128)(2,1)} %collective-permute-done.19.refs_14_), channel_id=1, source_target_pairs={{0,64},{1,17},{16,80},{17,33},{32,96},{33,49},{48,112},{49,1},{64,... | collective-permute-start | bytes 1572872 | tf_op jit(solution)/shard_map/ppermute | solution.py:35
  84.7 18.2 %collective-permute-start.22 = (bf16[8,2,128,128]{3,2,1,0:T(8,128)(2,1)}, bf16[8,2,128,128]{3,2,1,0:T(8,128)(2,1)}, u32[]{:S(2)}, u32[]{:S(2)}) collective-permute-start(bf16[8,2,128,128]{3,2,1,0:T(8,128)(2,1)} %collective-permute-done.21.refs_15_), channel_id=1, source_target_pairs={{0,64},{1,17},{16,80},{17,33},{32,96},{33,49},{48,112},{49,1},{64,... | collective-permute-start | bytes 1572872 | tf_op jit(solution)/shard_map/ppermute | solution.py:35
  115.7 14.3 %collective-permute-start = (bf16[8,2,128,128]{3,2,1,0:T(8,128)(2,1)S(1)}, bf16[8,2,128,128]{3,2,1,0:T(8,128)(2,1)S(1)}, u32[]{:S(2)}, u32[]{:S(2)}) collective-permute-start(bf16[8,2,128,128]{3,2,1,0:T(8,128)(2,1)S(1)} %get-tuple-element.20.refs_0_), channel_id=1, source_target_pairs={{0,48},{1,193},{16,0},{17,209},{32,16},{33,225},{48,32},{49,241},{... | collective-permute-start | bytes 1572872 | tf_op jit(solution)/shard_map/cond/branch_0_fun/ppermute | solution.py:35
  118.2 11.7 %collective-permute-start.1 = (bf16[8,2,128,128]{3,2,1,0:T(8,128)(2,1)S(1)}, bf16[8,2,128,128]{3,2,1,0:T(8,128)(2,1)S(1)}, u32[]{:S(2)}, u32[]{:S(2)}) collective-permute-start(bf16[8,2,128,128]{3,2,1,0:T(8,128)(2,1)S(1)} %get-tuple-element.20.refs_0_), channel_id=1, source_target_pairs={{0,32},{1,129},{16,48},{17,145},{32,0},{33,161},{48,16},{49,177},{... | collective-permute-start | bytes 1572872 | tf_op jit(solution)/shard_map/cond/branch_0_fun/ppermute | solution.py:35
  118.9 14.8 %collective-permute-start.2 = (bf16[8,2,128,128]{3,2,1,0:T(8,128)(2,1)S(1)}, bf16[8,2,128,128]{3,2,1,0:T(8,128)(2,1)S(1)}, u32[]{:S(2)}, u32[]{:S(2)}) collective-permute-start(bf16[8,2,128,128]{3,2,1,0:T(8,128)(2,1)S(1)} %get-tuple-element.20.refs_0_), channel_id=1, source_target_pairs={{0,16},{1,65},{16,32},{17,81},{32,48},{33,97},{48,0},{49,113},{64,... | collective-permute-start | bytes 1572872 | tf_op jit(solution)/shard_map/cond/branch_0_fun/ppermute | solution.py:35
  130.0 3.7 %copy-start.1 = (bf16[8,2,128,128]{3,2,1,0:T(8,128)(2,1)}, bf16[8,2,128,128]{3,2,1,0:T(8,128)(2,1)S(1)}, u32[]{:S(2)}) copy-start(bf16[8,2,128,128]{3,2,1,0:T(8,128)(2,1)S(1)} %collective-permute-done.refs_1_) | copy-start | bytes 1572868 | tf_op jit(solution)/shard_map/cond
  130.0 3.7 %copy-start.2 = (bf16[8,2,128,128]{3,2,1,0:T(8,128)(2,1)}, bf16[8,2,128,128]{3,2,1,0:T(8,128)(2,1)S(1)}, u32[]{:S(2)}) copy-start(bf16[8,2,128,128]{3,2,1,0:T(8,128)(2,1)S(1)} %collective-permute-done.1.refs_2_) | copy-start | bytes 1572868 | tf_op jit(solution)/shard_map/cond
  133.7 0.8 copy-start.3
  137.5 9.8 %collective-permute-start.3 = (bf16[8,2,128,128]{3,2,1,0:T(8,128)(2,1)}, bf16[8,2,128,128]{3,2,1,0:T(8,128)(2,1)S(1)}, u32[]{:S(2)}, u32[]{:S(2)}) collective-permute-start(bf16[8,2,128,128]{3,2,1,0:T(8,128)(2,1)} %get-tuple-element.22), channel_id=1, source_target_pairs={{0,64},{1,17},{16,80},{17,33},{32,96},{33,49},{48,112},{49,1},{64,... | collective-permute-start | bytes 1572872 | tf_op jit(solution)/shard_map/cond/branch_0_fun/ppermute | solution.py:35
  138.2 15.0 %collective-permute-start.4 = (bf16[8,2,128,128]{3,2,1,0:T(8,128)(2,1)}, bf16[8,2,128,128]{3,2,1,0:T(8,128)(2,1)S(1)}, u32[]{:S(2)}, u32[]{:S(2)}) collective-permute-start(bf16[8,2,128,128]{3,2,1,0:T(8,128)(2,1)} %get-tuple-element.23), channel_id=1, source_target_pairs={{0,128},{1,33},{16,144},{17,49},{32,160},{33,1},{48,176},{49,17},{... | collective-permute-start | bytes 1572872 | tf_op jit(solution)/shard_map/cond/branch_0_fun/ppermute | solution.py:35
  140.5 13.0 %collective-permute-start.5 = (bf16[8,2,128,128]{3,2,1,0:T(8,128)(2,1)}, bf16[8,2,128,128]{3,2,1,0:T(8,128)(2,1)S(1)}, u32[]{:S(2)}, u32[]{:S(2)}) collective-permute-start(bf16[8,2,128,128]{3,2,1,0:T(8,128)(2,1)} %get-tuple-element.24), channel_id=1, source_target_pairs={{0,192},{1,49},{16,208},{17,1},{32,224},{33,17},{48,240},{49,33},{... | collective-permute-start | bytes 1572872 | tf_op jit(solution)/shard_map/cond/branch_0_fun/ppermute | solution.py:35
  147.3 6.2 %copy-start.9 = (bf16[8,2,128,128]{3,2,1,0:T(8,128)(2,1)}, bf16[8,2,128,128]{3,2,1,0:T(8,128)(2,1)S(1)}, u32[]{:S(2)}) copy-start(bf16[8,2,128,128]{3,2,1,0:T(8,128)(2,1)S(1)} %collective-permute-done.3.refs_4_) | copy-start | bytes 1572868 | tf_op jit(solution)/shard_map/cond
  153.2 0.8 copy-start.10
  153.5 0.8 copy-start.11
  157.2 3.6 %collective-permute-start.25 = (bf16[8,128,128]{2,1,0:T(8,128)(2,1)S(1)}, bf16[8,128,128]{2,1,0:T(8,128)(2,1)S(1)}, u32[]{:S(2)}, u32[]{:S(2)}) collective-permute-start(bf16[8,128,128]{2,1,0:T(8,128)(2,1)S(1)} %get-tuple-element.48), channel_id=1, source_target_pairs={{0,1},{1,0},{2,3},{3,2},{4,5},{5,4},{6,7},{7,6},{8,9},{9,8},{10,11... | collective-permute-start | bytes 786440 | tf_op jit(solution)/shard_map/ppermute | solution.py:39
  159.6 2.0 %collective-permute-start.26 = (bf16[8,128,128]{2,1,0:T(8,128)(2,1)S(1)}, bf16[8,128,128]{2,1,0:T(8,128)(2,1)S(1)}, u32[]{:S(2)}, u32[]{:S(2)}) collective-permute-start(bf16[8,128,128]{2,1,0:T(8,128)(2,1)S(1)} %get-tuple-element.49), channel_id=1, source_target_pairs={{0,1},{1,0},{2,3},{3,2},{4,5},{5,4},{6,7},{7,6},{8,9},{9,8},{10,11... | collective-permute-start | bytes 786440 | tf_op jit(solution)/shard_map/ppermute | solution.py:39
Sparse Core Ops, SparseCore 0:
  9.8 102.4 all-gather.4

commit v2 on v1

--- a/solution.py
+++ b/solution.py
@@ -45,8 +45,9 @@
 
     def issue(entry, carry):
         chunk, i = lax.shift_right_logical(entry, 2), entry & 3
-        source = ham.at[table[HAM_AT + entry]]
-        pltpu.make_async_copy(source, ham_buf.at[chunk, i], sems.at[0, chunk]).start()
+        for kind in range(2):
+            source = ham.at[table[HAM_AT + entry] + 16 * kind]
+            pltpu.make_async_copy(source, ham_buf.at[chunk, i, kind], sems.at[0, chunk]).start()
         place = table[PLACE_AT + entry]
 
         def copy(ref, index):
@@ -204,7 +205,7 @@
             counts[4] = n + 1
             sparse = jnp.where(sender == 0, near, (sender + 3) * 8 + rank)
             places = (((4 - sender) & 3) * 32 + near, sparse, lax.shift_right_logical(slot, 2) * 8 + index)
-            put(n, (q * 2 + group) * 16 + row, lax.shift_right_logical(i, 3), places)
+            put(n, (q * 2 + group) * 32 + row, lax.shift_right_logical(i, 3), places)
 
         return carry
 
@@ -298,7 +299,7 @@
     def paired(cheb, tang):
         return jnp.stack([mine(cheb).reshape(8, 128, 128), mine(tang).reshape(8, 128, 128)], axis=1)
 
-    ham_pair = jnp.stack([ham_blocks[:, 0], deriv_blocks[:, 0]], axis=1)
+    ham_pair = jnp.concatenate([ham_blocks[:, 0], deriv_blocks[:, 0]])
     ham = lax.all_gather(ham_pair, ("col", "depth"), axis=0, tiled=True)
 
     other_cols = swap(ham_cols)

time: 170 us -> 170 us (level)
    another operation x1 -> x0, other arithmetic: 2.32 us -> none  [on_device(): ham_pair = jnp.stack([ham_blocks[:, 0], deriv_blocks[:, 0]], axis=1)]
    concatenate x0 -> x1, other arithmetic: none -> 2.31 us  [on_device(): ham_pair = jnp.concatenate([ham_blocks[:, 0], deriv_blocks[:, 0]])]
where the time goes in v2:
time: 170 us; the launch traced here: 169 us
  waiting for transfers between devices  69.8 us (41%)
  starting transfers between devices  48.5 us (29%)
  Pallas kernels  23.5 us (14%)
  between operations  14.8 us (9%)
  local copies, waits for them, and re-layouts  6.66 us (4%)
  other arithmetic  5.98 us (4%)
    ppermute x24, waiting for transfers between devices, shift_side(): return lax.ppermute(array, ('row', 'depth'), side_ring(shift, second))  54 us
    ppermute x24, starting transfers between devices, shift_side(): return lax.ppermute(array, ('row', 'depth'), side_ring(shift, second))  25.5 us
    all_to_all x1, starting transfers between devices, on_device(): lax.all_to_all(jnp.broadcast_to(overflow, (256, 1, 128)), AXES, 0, 0, til...  17.4 us
    all_gather x1, waiting for transfers between devices, on_device(): ham = lax.all_gather(ham_pair, ('col', 'depth'), axis=0, tiled=True)  9.49 us
    pallas_call x1, Pallas kernels, sends(): pl.pallas_call(sends_kernel, out_shape=jax.ShapeDtypeStruct((32,), jnp.in...  9.22 us
    pallas_call x2, Pallas kernels, combine(): pl.pallas_call(functools.partial(combine_kernel, len(panels), apart), out...  6.19 us
    ppermute x3, starting transfers between devices, swap(): return lax.ppermute(array, 'depth', [(0, 1), (1, 0)])  5.55 us
    all_to_all x1, waiting for transfers between devices, on_device(): lax.all_to_all(jnp.broadcast_to(overflow, (256, 1, 128)), AXES, 0, 0, til...  5.17 us
  transfers between devices with their start and end apart: 29, of which 16 were waited for; matrix products, arithmetic and copies ran while one was open for 5% of the time, Pallas kernels for 8%

profile of v2, /device:TPU:1, one launch (start us, length us, event | category | flops | bytes accessed | tf_op | source)
XLA Modules:
  0.0 169.2 jit_solution(7821958732069590966)
XLA Ops:
  7.2 2.3 %pad_maximum_fusion = bf16[32,128,128]{2,1,0:T(8,128)(2,1)} fusion(bf16[16,128,128]{2,1,0:T(8,128)(2,1)} %bitcast.23, bf16[16,128,128]{2,1,0:T(8,128)(2,1)} %bitcast.24), kind=kLoop, calls=%fused_computation | loop fusion | flops 524288 | bytes 2097152 | tf_op jit(solution)/shard_map/concatenate | solution.py:302
  9.5 0.8 copy.22.cols
  10.3 3.2 %collective-permute-start.7 = (s32[16,8]{1,0:T(8,128)S(1)}, s32[16,8]{1,0:T(8,128)S(1)}, u32[]{:S(2)}, u32[]{:S(2)}) collective-permute-start(s32[16,8]{1,0:T(8,128)S(1)} %copy.22.cols), channel_id=1, source_target_pairs={{0,1},{1,0},{2,3},{3,2},{4,5},{5,4},{6,7},{7,6},{8,9},{9,8},{10,11... | collective-permute-start | bytes 1544 | tf_op jit(solution)/shard_map/ppermute | solution.py:39
  13.5 1.1 constant_dynamic-slice_fusion.2
  14.6 0.8 reshape.14
  15.4 0.8 collective-permute-start.8
  17.4 2.8 %collective-permute-start.11 = (bf16[8,2,128,128]{3,2,1,0:T(8,128)(2,1)S(1)}, bf16[8,2,128,128]{3,2,1,0:T(8,128)(2,1)S(1)}, u32[]{:S(2)}, u32[]{:S(2)}) collective-permute-start(bf16[8,2,128,128]{3,2,1,0:T(8,128)(2,1)S(1)} %pad_maximum_fusion.1.refs_0_), channel_id=1, source_target_pairs={{0,48},{1,193},{16,0},{17,209},{32,16},{33,225},{48,32},{49,241},{... | collective-permute-start | bytes 1572872 | tf_op jit(solution)/shard_map/ppermute | solution.py:35
  20.6 0.7 collective-permute-start.13
  21.3 2.1 %collective-permute-start.6 = (bf16[8,2,128,128]{3,2,1,0:T(8,128)(2,1)S(1)}, bf16[8,2,128,128]{3,2,1,0:T(8,128)(2,1)S(1)}, u32[]{:S(2)}, u32[]{:S(2)}) collective-permute-start(bf16[8,2,128,128]{3,2,1,0:T(8,128)(2,1)S(1)} %pad_maximum_fusion.1.refs_0_), channel_id=1, source_target_pairs={{0,192},{1,49},{16,208},{17,1},{32,224},{33,17},{48,240},{49,33},{... | collective-permute-start | bytes 1572872 | tf_op jit(solution)/shard_map/ppermute | solution.py:35
  23.3 6.6 %collective-permute-done.11.refs_1_ = bf16[8,2,128,128]{3,2,1,0:T(8,128)(2,1)S(1)} collective-permute-done((bf16[8,2,128,128]{3,2,1,0:T(8,128)(2,1)S(1)}, bf16[8,2,128,128]{3,2,1,0:T(8,128)(2,1)S(1)}, u32[]{:S(2)}, u32[]{:S(2)}) %collective-permute-start.11) | collective-permute-done | bytes 524320 | tf_op jit(solution)/shard_map/ppermute | solution.py:35
  30.0 2.1 %collective-permute-start.14 = (bf16[8,2,128,128]{3,2,1,0:T(8,128)(2,1)S(1)}, bf16[8,2,128,128]{3,2,1,0:T(8,128)(2,1)}, u32[]{:S(2)}, u32[]{:S(2)}) collective-permute-start(bf16[8,2,128,128]{3,2,1,0:T(8,128)(2,1)S(1)} %collective-permute-done.11.refs_1_), channel_id=1, source_target_pairs={{0,192},{1,49},{16,208},{17,1},{32,224},{33,17},{48,240},{49,33},{... | collective-permute-start | bytes 1572872 | tf_op jit(solution)/shard_map/ppermute | solution.py:35
  32.1 2.0 %collective-permute-start.15 = (bf16[8,2,128,128]{3,2,1,0:T(8,128)(2,1)S(1)}, bf16[8,2,128,128]{3,2,1,0:T(8,128)(2,1)}, u32[]{:S(2)}, u32[]{:S(2)}) collective-permute-start(bf16[8,2,128,128]{3,2,1,0:T(8,128)(2,1)S(1)} %collective-permute-done.12.refs_2_), channel_id=1, source_target_pairs={{0,192},{1,49},{16,208},{17,1},{32,224},{33,17},{48,240},{49,33},{... | collective-permute-start | bytes 1572872 | tf_op jit(solution)/shard_map/ppermute | solution.py:35
  34.1 6.4 %collective-permute-done.13.refs_3_ = bf16[8,2,128,128]{3,2,1,0:T(8,128)(2,1)S(1)} collective-permute-done((bf16[8,2,128,128]{3,2,1,0:T(8,128)(2,1)S(1)}, bf16[8,2,128,128]{3,2,1,0:T(8,128)(2,1)S(1)}, u32[]{:S(2)}, u32[]{:S(2)}) %collective-permute-start.13) | collective-permute-done | bytes 524320 | tf_op jit(solution)/shard_map/ppermute | solution.py:35
  40.5 2.1 %collective-permute-start.16 = (bf16[8,2,128,128]{3,2,1,0:T(8,128)(2,1)S(1)}, bf16[8,2,128,128]{3,2,1,0:T(8,128)(2,1)}, u32[]{:S(2)}, u32[]{:S(2)}) collective-permute-start(bf16[8,2,128,128]{3,2,1,0:T(8,128)(2,1)S(1)} %collective-permute-done.13.refs_3_), channel_id=1, source_target_pairs={{0,192},{1,49},{16,208},{17,1},{32,224},{33,17},{48,240},{49,33},{... | collective-permute-start | bytes 1572872 | tf_op jit(solution)/shard_map/ppermute | solution.py:35
  43.5 4.9 %shard_map.104 = (s32[208]{0:T(256)}, s32[208]{0:T(256)S(1)}, s32[208]{0:T(256)S(1)}, s32[1]{0:T(128)}) custom-call(s32[4,64]{1,0:T(4,128)} %rows.3, s32[16,8]{1,0:T(8,128)} %copy-done.12, s32[16,8]{1,0:T(8,128)} %copy-done.13, s32[4,4]{1,0:T(4,128)} %keep.1), custom_call_target="tpu_custom_call" | custom-call | tf_op jit(solution)/shard_map/pallas_call | solution.py:230
  48.5 1.3 broadcast_in_dim.2
  49.8 17.4 %all-to-all-start = ((s32[256,1,128]{2,1,0:T(1,128)}), s32[256,1,128]{2,1,0:T(1,128)S(1)}, u32[]{:S(2)}, u32[]{:S(2)}) async-start(s32[256,1,128]{2,1,0:T(1,128)} %broadcast_in_dim.2), calls=%async_computation | async-start | bytes 262144 | tf_op jit(solution)/shard_map/all_to_all | solution.py:307
  67.2 9.2 %shard_map.105 = s32[32]{0:T(128)S(1)} custom-call(s32[4,64]{1,0:T(4,128)} %rows.3, s32[34,8]{1,0:T(8,128)} %copy-done.14, s32[34,8]{1,0:T(8,128)} %copy-done.15, s32[34,8]{1,0:T(8,128)} %copy-done.16), custom_call_target="tpu_custom_call" | custom-call | tf_op jit(solution)/shard_map/pallas_call | solution.py:274
  76.5 5.2 %all-to-all-done = s32[256,1,128]{2,1,0:T(1,128)S(1)} async-done(((s32[256,1,128]{2,1,0:T(1,128)}), s32[256,1,128]{2,1,0:T(1,128)S(1)}, u32[]{:S(2)}, u32[]{:S(2)}) %all-to-all-start) | async-done | bytes 131104 | tf_op jit(solution)/shard_map/all_to_all | solution.py:307
  81.9 1.2 collective-permute-start.24
  83.1 1.5 collective-permute-start.18
  84.7 1.1 constant_dynamic-slice_fusion
  85.8 0.9 pad_maximum_fusion.2.refs_16_
  86.7 0.9 reduce_max.9
  88.3 1.8 %collective-permute-done.17.refs_8_ = bf16[8,2,128,128]{3,2,1,0:T(8,128)(2,1)} collective-permute-done((bf16[8,2,128,128]{3,2,1,0:T(8,128)(2,1)S(1)}, bf16[8,2,128,128]{3,2,1,0:T(8,128)(2,1)}, u32[]{:S(2)}, u32[]{:S(2)}) %collective-permute-start.17) | collective-permute-done | bytes 524320 | tf_op jit(solution)/shard_map/ppermute | solution.py:35
  90.1 1.5 collective-permute-done.24.refs_13_
  91.6 4.1 %collective-permute-done.18.refs_9_ = bf16[8,2,128,128]{3,2,1,0:T(8,128)(2,1)} collective-permute-done((bf16[8,2,128,128]{3,2,1,0:T(8,128)(2,1)}, bf16[8,2,128,128]{3,2,1,0:T(8,128)(2,1)}, u32[]{:S(2)}, u32[]{:S(2)}) %collective-permute-start.18) | collective-permute-done | bytes 524320 | tf_op jit(solution)/shard_map/ppermute | solution.py:35
  95.7 1.5 collective-permute-done.20.refs_10_
  97.2 5.6 %collective-permute-done.22.refs_11_ = bf16[8,2,128,128]{3,2,1,0:T(8,128)(2,1)} collective-permute-done((bf16[8,2,128,128]{3,2,1,0:T(8,128)(2,1)}, bf16[8,2,128,128]{3,2,1,0:T(8,128)(2,1)}, u32[]{:S(2)}, u32[]{:S(2)}) %collective-permute-start.22) | collective-permute-done | bytes 524320 | tf_op jit(solution)/shard_map/ppermute | solution.py:35
  102.8 9.5 %all-gather.5.cloned.1.call-done.ham = bf16[512,128,128]{2,1,0:T(8,128)(2,1)} async-done(((bf16[32,128,128]{2,1,0:T(8,128)(2,1)}), bf16[512,128,128]{2,1,0:T(8,128)(2,1)}) %all-gather.5.cloned.1.call-update) | async-done | bytes 16777232 | tf_op jit(solution)/shard_map/all_gather | solution.py:303
  112.3 3.4 %shard_map.106 = bf16[8,2,128,128]{3,2,1,0:T(8,128)(2,1)S(1)} custom-call(s32[208]{0:T(256)} %get-tuple-element.43.table, bf16[512,128,128]{2,1,0:T(8,128)(2,1)} %all-gather.5.cloned.1.call-done.ham, bf16[8,2,128,128]{3,2,1,0:T(8,128)(2,1)S(1)} %pad_maximum_fusion.1.refs_0_, bf16[8,2,128,128]{3,2,1,0:T(8,128)(2,1)} %copy-done.4, ...), custom_call_target="tpu_custom_call" | custom-call | flops 1073741824 | bytes 8388608 | tf_op jit(solution)/shard_map/pallas_call | solution.py:97
  115.7 41.5 %conditional.1 = ((bf16[8,128,128]{2,1,0:T(8,128)(2,1)S(1)}, bf16[8,128,128]{2,1,0:T(8,128)(2,1)S(1)})) conditional(s32[]{:T(128)} %convert_element_type.3, (bf16[8,2,128,128]{3,2,1,0:T(8,128)(2,1)S(1)}, s32[32]{0:T(128)S(1)}, s32[208]{0:T(256)S(1)}, bf16[512,128,128]{2,1,0:T(8,128)(2,1)}, bf16[8,2,128,128]{3,2,1,0:T(8,128)(2,1)S(1)}) %tuple.16, ...), branch_computations={%region_1.0_spmd, %region_2.0_spmd} | conditional | flops 1073741824 | bytes 37749152 | solution.py:337
  115.7 2.5 %collective-permute-start = (bf16[8,2,128,128]{3,2,1,0:T(8,128)(2,1)S(1)}, bf16[8,2,128,128]{3,2,1,0:T(8,128)(2,1)S(1)}, u32[]{:S(2)}, u32[]{:S(2)}) collective-permute-start(bf16[8,2,128,128]{3,2,1,0:T(8,128)(2,1)S(1)} %get-tuple-element.20.refs_0_), channel_id=1, source_target_pairs={{0,48},{1,193},{16,0},{17,209},{32,16},{33,225},{48,32},{49,241},{... | collective-permute-start | bytes 1572872 | tf_op jit(solution)/shard_map/cond/branch_0_fun/ppermute | solution.py:35
  118.4 0.8 collective-permute-start.2
  119.2 10.8 %collective-permute-done.refs_1_ = bf16[8,2,128,128]{3,2,1,0:T(8,128)(2,1)S(1)} collective-permute-done((bf16[8,2,128,128]{3,2,1,0:T(8,128)(2,1)S(1)}, bf16[8,2,128,128]{3,2,1,0:T(8,128)(2,1)S(1)}, u32[]{:S(2)}, u32[]{:S(2)}) %collective-permute-start) | collective-permute-done | bytes 524320 | tf_op jit(solution)/shard_map/cond/branch_0_fun/ppermute | solution.py:35
  130.0 3.6 %collective-permute-done.2.refs_3_ = bf16[8,2,128,128]{3,2,1,0:T(8,128)(2,1)S(1)} collective-permute-done((bf16[8,2,128,128]{3,2,1,0:T(8,128)(2,1)S(1)}, bf16[8,2,128,128]{3,2,1,0:T(8,128)(2,1)S(1)}, u32[]{:S(2)}, u32[]{:S(2)}) %collective-permute-start.2) | collective-permute-done | bytes 524320 | tf_op jit(solution)/shard_map/cond/branch_0_fun/ppermute | solution.py:35
  133.6 0.8 copy-done.3
  134.4 3.1 %branch_0_fun.2 = (bf16[8,2,128,128]{3,2,1,0:T(8,128)(2,1)}, bf16[8,2,128,128]{3,2,1,0:T(8,128)(2,1)}, bf16[8,2,128,128]{3,2,1,0:T(8,128)(2,1)}) custom-call(s32[32]{0:T(128)S(1)} %get-tuple-element.21.table, bf16[8,2,128,128]{3,2,1,0:T(8,128)(2,1)S(1)} %get-tuple-element.20.refs_0_, bf16[8,2,128,128]{3,2,1,0:T(8,128)(2,1)} %copy-done.1, ...), custom_call_target="tpu_custom_call" | custom-call | bytes 4194304 | tf_op jit(solution)/shard_map/cond/branch_0_fun/pallas_call | solution.py:141
  137.5 1.0 collective-permute-start.3
  138.5 2.2 %collective-permute-start.4 = (bf16[8,2,128,128]{3,2,1,0:T(8,128)(2,1)}, bf16[8,2,128,128]{3,2,1,0:T(8,128)(2,1)S(1)}, u32[]{:S(2)}, u32[]{:S(2)}) collective-permute-start(bf16[8,2,128,128]{3,2,1,0:T(8,128)(2,1)} %get-tuple-element.23), channel_id=1, source_target_pairs={{0,128},{1,33},{16,144},{17,49},{32,160},{33,1},{48,176},{49,17},{... | collective-permute-start | bytes 1572872 | tf_op jit(solution)/shard_map/cond/branch_0_fun/ppermute | solution.py:35
  140.7 1.4 collective-permute-start.5
  142.1 5.3 %collective-permute-done.3.refs_4_ = bf16[8,2,128,128]{3,2,1,0:T(8,128)(2,1)S(1)} collective-permute-done((bf16[8,2,128,128]{3,2,1,0:T(8,128)(2,1)}, bf16[8,2,128,128]{3,2,1,0:T(8,128)(2,1)S(1)}, u32[]{:S(2)}, u32[]{:S(2)}) %collective-permute-start.3) | collective-permute-done | bytes 524320 | tf_op jit(solution)/shard_map/cond/branch_0_fun/ppermute | solution.py:35
  147.3 6.1 %collective-permute-done.4.refs_5_ = bf16[8,2,128,128]{3,2,1,0:T(8,128)(2,1)S(1)} collective-permute-done((bf16[8,2,128,128]{3,2,1,0:T(8,128)(2,1)}, bf16[8,2,128,128]{3,2,1,0:T(8,128)(2,1)S(1)}, u32[]{:S(2)}, u32[]{:S(2)}) %collective-permute-start.4) | collective-permute-done | bytes 524320 | tf_op jit(solution)/shard_map/cond/branch_0_fun/ppermute | solution.py:35
  154.4 2.8 %branch_0_fun.3 = (bf16[8,128,128]{2,1,0:T(8,128)(2,1)S(1)}, bf16[8,128,128]{2,1,0:T(8,128)(2,1)S(1)}) custom-call(s32[208]{0:T(256)S(1)} %get-tuple-element.18.table, bf16[512,128,128]{2,1,0:T(8,128)(2,1)} %get-tuple-element.19.ham, bf16[8,2,128,128]{3,2,1,0:T(8,128)(2,1)S(1)} %get-tuple-element.20.refs_0_, bf16[8,2,128,128]{3,2,1,0:T(8,128)(2,1)} %copy-done.1, ...), custom_call_target="tpu_custom_call" | custom-call | flops 1073741824 | bytes 8388608 | tf_op jit(solution)/shard_map/cond/branch_0_fun/pallas_call | solution.py:97
  157.2 2.2 %collective-permute-start.25 = (bf16[8,128,128]{2,1,0:T(8,128)(2,1)S(1)}, bf16[8,128,128]{2,1,0:T(8,128)(2,1)S(1)}, u32[]{:S(2)}, u32[]{:S(2)}) collective-permute-start(bf16[8,128,128]{2,1,0:T(8,128)(2,1)S(1)} %get-tuple-element.48), channel_id=1, source_target_pairs={{0,1},{1,0},{2,3},{3,2},{4,5},{5,4},{6,7},{7,6},{8,9},{9,8},{10,11... | collective-permute-start | bytes 786440 | tf_op jit(solution)/shard_map/ppermute | solution.py:39
  159.5 1.1 collective-permute-done.25
  160.6 0.8 pad_maximum_fusion.3
  161.5 0.8 pad_maximum_fusion.4
  (63 shorter events, 4.3 us)
Async XLA Ops:
  7.2 105.1 %all-gather.5.cloned.1.call-start = ((), (), s32[]{:S(2)}) async-start(), calls=%async_computation.2 | async-start | bytes 17825792 | tf_op jit(solution)/shard_map/all_gather | solution.py:303
  10.3 33.2 %copy-start.12 = (s32[16,8]{1,0:T(8,128)}, s32[16,8]{1,0:T(8,128)S(1)}, u32[]{:S(2)}) copy-start(s32[16,8]{1,0:T(8,128)S(1)} %copy.22.cols) | copy-start | bytes 1540
  10.3 5.1 %collective-permute-start.7 = (s32[16,8]{1,0:T(8,128)S(1)}, s32[16,8]{1,0:T(8,128)S(1)}, u32[]{:S(2)}, u32[]{:S(2)}) collective-permute-start(s32[16,8]{1,0:T(8,128)S(1)} %copy.22.cols), channel_id=1, source_target_pairs={{0,1},{1,0},{2,3},{3,2},{4,5},{5,4},{6,7},{7,6},{8,9},{9,8},{10,11... | collective-permute-start | bytes 1544 | tf_op jit(solution)/shard_map/ppermute | solution.py:39
  15.4 28.2 %copy-start.13 = (s32[16,8]{1,0:T(8,128)}, s32[16,8]{1,0:T(8,128)S(1)}, u32[]{:S(2)}) copy-start(s32[16,8]{1,0:T(8,128)S(1)} %collective-permute-done.7.other_cols) | copy-start | bytes 1540
  15.4 5.2 %collective-permute-start.8 = (s32[34,8]{1,0:T(8,128)S(1)}, s32[34,8]{1,0:T(8,128)S(1)}, u32[]{:S(2)}, u32[]{:S(2)}) collective-permute-start(s32[34,8]{1,0:T(8,128)S(1)} %pad_add_fusion), channel_id=1, source_target_pairs={{0,192},{1,49},{16,208},{17,1},{32,224},{33,17},{48,240},{49,33},{... | collective-permute-start | bytes 3272 | tf_op jit(solution)/shard_map/ppermute | solution.py:35
  16.2 5.0 %collective-permute-start.9 = (s32[34,8]{1,0:T(8,128)S(1)}, s32[34,8]{1,0:T(8,128)S(1)}, u32[]{:S(2)}, u32[]{:S(2)}) collective-permute-start(s32[34,8]{1,0:T(8,128)S(1)} %pad_add_fusion), channel_id=1, source_target_pairs={{0,128},{1,33},{16,144},{17,49},{32,160},{33,1},{48,176},{49,17},{... | collective-permute-start | bytes 3272 | tf_op jit(solution)/shard_map/ppermute | solution.py:35
  16.7 6.6 %collective-permute-start.10 = (s32[34,8]{1,0:T(8,128)S(1)}, s32[34,8]{1,0:T(8,128)S(1)}, u32[]{:S(2)}, u32[]{:S(2)}) collective-permute-start(s32[34,8]{1,0:T(8,128)S(1)} %pad_add_fusion), channel_id=1, source_target_pairs={{0,64},{1,17},{16,80},{17,33},{32,96},{33,49},{48,112},{49,1},{64,... | collective-permute-start | bytes 3272 | tf_op jit(solution)/shard_map/ppermute | solution.py:35
  17.4 12.6 %collective-permute-start.11 = (bf16[8,2,128,128]{3,2,1,0:T(8,128)(2,1)S(1)}, bf16[8,2,128,128]{3,2,1,0:T(8,128)(2,1)S(1)}, u32[]{:S(2)}, u32[]{:S(2)}) collective-permute-start(bf16[8,2,128,128]{3,2,1,0:T(8,128)(2,1)S(1)} %pad_maximum_fusion.1.refs_0_), channel_id=1, source_target_pairs={{0,48},{1,193},{16,0},{17,209},{32,16},{33,225},{48,32},{49,241},{... | collective-permute-start | bytes 1572872 | tf_op jit(solution)/shard_map/ppermute | solution.py:35
  20.2 11.9 %collective-permute-start.12 = (bf16[8,2,128,128]{3,2,1,0:T(8,128)(2,1)S(1)}, bf16[8,2,128,128]{3,2,1,0:T(8,128)(2,1)S(1)}, u32[]{:S(2)}, u32[]{:S(2)}) collective-permute-start(bf16[8,2,128,128]{3,2,1,0:T(8,128)(2,1)S(1)} %pad_maximum_fusion.1.refs_0_), channel_id=1, source_target_pairs={{0,32},{1,129},{16,48},{17,145},{32,0},{33,161},{48,16},{49,177},{... | collective-permute-start | bytes 1572872 | tf_op jit(solution)/shard_map/ppermute | solution.py:35
  20.6 46.7 %copy-start.14 = (s32[34,8]{1,0:T(8,128)}, s32[34,8]{1,0:T(8,128)S(1)}, u32[]{:S(2)}) copy-start(s32[34,8]{1,0:T(8,128)S(1)} %collective-permute-done.8.refs_0_) | copy-start | bytes 3268
  20.6 20.0 %collective-permute-start.13 = (bf16[8,2,128,128]{3,2,1,0:T(8,128)(2,1)S(1)}, bf16[8,2,128,128]{3,2,1,0:T(8,128)(2,1)S(1)}, u32[]{:S(2)}, u32[]{:S(2)}) collective-permute-start(bf16[8,2,128,128]{3,2,1,0:T(8,128)(2,1)S(1)} %pad_maximum_fusion.1.refs_0_), channel_id=1, source_target_pairs={{0,16},{1,65},{16,32},{17,81},{32,48},{33,97},{48,0},{49,113},{64,... | collective-permute-start | bytes 1572872 | tf_op jit(solution)/shard_map/ppermute | solution.py:35
  21.3 46.0 %copy-start.15 = (s32[34,8]{1,0:T(8,128)}, s32[34,8]{1,0:T(8,128)S(1)}, u32[]{:S(2)}) copy-start(s32[34,8]{1,0:T(8,128)S(1)} %collective-permute-done.9.refs_1_) | copy-start | bytes 3268
  21.3 21.3 %collective-permute-start.6 = (bf16[8,2,128,128]{3,2,1,0:T(8,128)(2,1)S(1)}, bf16[8,2,128,128]{3,2,1,0:T(8,128)(2,1)S(1)}, u32[]{:S(2)}, u32[]{:S(2)}) collective-permute-start(bf16[8,2,128,128]{3,2,1,0:T(8,128)(2,1)S(1)} %pad_maximum_fusion.1.refs_0_), channel_id=1, source_target_pairs={{0,192},{1,49},{16,208},{17,1},{32,224},{33,17},{48,240},{49,33},{... | collective-permute-start | bytes 1572872 | tf_op jit(solution)/shard_map/ppermute | solution.py:35
  23.3 43.9 %copy-start.16 = (s32[34,8]{1,0:T(8,128)}, s32[34,8]{1,0:T(8,128)S(1)}, u32[]{:S(2)}) copy-start(s32[34,8]{1,0:T(8,128)S(1)} %collective-permute-done.10.refs_2_) | copy-start | bytes 3268
  23.3 19.8 %collective-permute-start.23 = (bf16[8,2,128,128]{3,2,1,0:T(8,128)(2,1)S(1)}, bf16[8,2,128,128]{3,2,1,0:T(8,128)(2,1)S(1)}, u32[]{:S(2)}, u32[]{:S(2)}) collective-permute-start(bf16[8,2,128,128]{3,2,1,0:T(8,128)(2,1)S(1)} %pad_maximum_fusion.1.refs_0_), channel_id=1, source_target_pairs={{0,64},{1,17},{16,80},{17,33},{32,96},{33,49},{48,112},{49,1},{64,... | collective-permute-start | bytes 1572872 | tf_op jit(solution)/shard_map/ppermute | solution.py:35
  30.0 82.3 %copy-start.4 = (bf16[8,2,128,128]{3,2,1,0:T(8,128)(2,1)}, bf16[8,2,128,128]{3,2,1,0:T(8,128)(2,1)S(1)}, u32[]{:S(2)}) copy-start(bf16[8,2,128,128]{3,2,1,0:T(8,128)(2,1)S(1)} %collective-permute-done.11.refs_1_) | copy-start | bytes 1572868
  30.0 51.6 %collective-permute-start.14 = (bf16[8,2,128,128]{3,2,1,0:T(8,128)(2,1)S(1)}, bf16[8,2,128,128]{3,2,1,0:T(8,128)(2,1)}, u32[]{:S(2)}, u32[]{:S(2)}) collective-permute-start(bf16[8,2,128,128]{3,2,1,0:T(8,128)(2,1)S(1)} %collective-permute-done.11.refs_1_), channel_id=1, source_target_pairs={{0,192},{1,49},{16,208},{17,1},{32,224},{33,17},{48,240},{49,33},{... | collective-permute-start | bytes 1572872 | tf_op jit(solution)/shard_map/ppermute | solution.py:35
  32.1 80.2 %copy-start.5 = (bf16[8,2,128,128]{3,2,1,0:T(8,128)(2,1)}, bf16[8,2,128,128]{3,2,1,0:T(8,128)(2,1)S(1)}, u32[]{:S(2)}) copy-start(bf16[8,2,128,128]{3,2,1,0:T(8,128)(2,1)S(1)} %collective-permute-done.12.refs_2_) | copy-start | bytes 1572868
  32.1 49.9 %collective-permute-start.15 = (bf16[8,2,128,128]{3,2,1,0:T(8,128)(2,1)S(1)}, bf16[8,2,128,128]{3,2,1,0:T(8,128)(2,1)}, u32[]{:S(2)}, u32[]{:S(2)}) collective-permute-start(bf16[8,2,128,128]{3,2,1,0:T(8,128)(2,1)S(1)} %collective-permute-done.12.refs_2_), channel_id=1, source_target_pairs={{0,192},{1,49},{16,208},{17,1},{32,224},{33,17},{48,240},{49,33},{... | collective-permute-start | bytes 1572872 | tf_op jit(solution)/shard_map/ppermute | solution.py:35
  40.5 71.8 %copy-start.6 = (bf16[8,2,128,128]{3,2,1,0:T(8,128)(2,1)}, bf16[8,2,128,128]{3,2,1,0:T(8,128)(2,1)S(1)}, u32[]{:S(2)}) copy-start(bf16[8,2,128,128]{3,2,1,0:T(8,128)(2,1)S(1)} %collective-permute-done.13.refs_3_) | copy-start | bytes 1572868
  40.5 42.6 %collective-permute-start.16 = (bf16[8,2,128,128]{3,2,1,0:T(8,128)(2,1)S(1)}, bf16[8,2,128,128]{3,2,1,0:T(8,128)(2,1)}, u32[]{:S(2)}, u32[]{:S(2)}) collective-permute-start(bf16[8,2,128,128]{3,2,1,0:T(8,128)(2,1)S(1)} %collective-permute-done.13.refs_3_), channel_id=1, source_target_pairs={{0,192},{1,49},{16,208},{17,1},{32,224},{33,17},{48,240},{49,33},{... | collective-permute-start | bytes 1572872 | tf_op jit(solution)/shard_map/ppermute | solution.py:35
  42.6 69.7 %copy-start.7 = (bf16[8,2,128,128]{3,2,1,0:T(8,128)(2,1)}, bf16[8,2,128,128]{3,2,1,0:T(8,128)(2,1)S(1)}, u32[]{:S(2)}) copy-start(bf16[8,2,128,128]{3,2,1,0:T(8,128)(2,1)S(1)} %collective-permute-done.6.refs_4_) | copy-start | bytes 1572868
  42.6 42.0 %collective-permute-start.19 = (bf16[8,2,128,128]{3,2,1,0:T(8,128)(2,1)S(1)}, bf16[8,2,128,128]{3,2,1,0:T(8,128)(2,1)}, u32[]{:S(2)}, u32[]{:S(2)}) collective-permute-start(bf16[8,2,128,128]{3,2,1,0:T(8,128)(2,1)S(1)} %collective-permute-done.12.refs_2_), channel_id=1, source_target_pairs={{0,64},{1,17},{16,80},{17,33},{32,96},{33,49},{48,112},{49,1},{64,... | collective-permute-start | bytes 1572872 | tf_op jit(solution)/shard_map/ppermute | solution.py:35
  43.1 69.2 %copy-start.8 = (bf16[8,2,128,128]{3,2,1,0:T(8,128)(2,1)}, bf16[8,2,128,128]{3,2,1,0:T(8,128)(2,1)S(1)}, u32[]{:S(2)}) copy-start(bf16[8,2,128,128]{3,2,1,0:T(8,128)(2,1)S(1)} %collective-permute-done.23.refs_12_) | copy-start | bytes 1572868
  43.1 41.5 %collective-permute-start.21 = (bf16[8,2,128,128]{3,2,1,0:T(8,128)(2,1)S(1)}, bf16[8,2,128,128]{3,2,1,0:T(8,128)(2,1)}, u32[]{:S(2)}, u32[]{:S(2)}) collective-permute-start(bf16[8,2,128,128]{3,2,1,0:T(8,128)(2,1)S(1)} %collective-permute-done.13.refs_3_), channel_id=1, source_target_pairs={{0,64},{1,17},{16,80},{17,33},{32,96},{33,49},{48,112},{49,1},{64,... | collective-permute-start | bytes 1572872 | tf_op jit(solution)/shard_map/ppermute | solution.py:35
  49.8 31.8 %all-to-all-start = ((s32[256,1,128]{2,1,0:T(1,128)}), s32[256,1,128]{2,1,0:T(1,128)S(1)}, u32[]{:S(2)}, u32[]{:S(2)}) async-start(s32[256,1,128]{2,1,0:T(1,128)} %broadcast_in_dim.2), calls=%async_computation | async-start | bytes 262144 | tf_op jit(solution)/shard_map/all_to_all | solution.py:307
  81.6 8.4 %collective-permute-start.17 = (bf16[8,2,128,128]{3,2,1,0:T(8,128)(2,1)S(1)}, bf16[8,2,128,128]{3,2,1,0:T(8,128)(2,1)}, u32[]{:S(2)}, u32[]{:S(2)}) collective-permute-start(bf16[8,2,128,128]{3,2,1,0:T(8,128)(2,1)S(1)} %collective-permute-done.6.refs_4_), channel_id=1, source_target_pairs={{0,192},{1,49},{16,208},{17,1},{32,224},{33,17},{48,240},{49,33},{... | collective-permute-start | bytes 1572872 | tf_op jit(solution)/shard_map/ppermute | solution.py:35
  81.9 9.6 %collective-permute-start.24 = (bf16[8,2,128,128]{3,2,1,0:T(8,128)(2,1)S(1)}, bf16[8,2,128,128]{3,2,1,0:T(8,128)(2,1)}, u32[]{:S(2)}, u32[]{:S(2)}) collective-permute-start(bf16[8,2,128,128]{3,2,1,0:T(8,128)(2,1)S(1)} %collective-permute-done.11.refs_1_), channel_id=1, source_target_pairs={{0,64},{1,17},{16,80},{17,33},{32,96},{33,49},{48,112},{49,1},{64,... | collective-permute-start | bytes 1572872 | tf_op jit(solution)/shard_map/ppermute | solution.py:35
  83.1 12.6 %collective-permute-start.18 = (bf16[8,2,128,128]{3,2,1,0:T(8,128)(2,1)}, bf16[8,2,128,128]{3,2,1,0:T(8,128)(2,1)}, u32[]{:S(2)}, u32[]{:S(2)}) collective-permute-start(bf16[8,2,128,128]{3,2,1,0:T(8,128)(2,1)} %collective-permute-done.14.refs_5_), channel_id=1, source_target_pairs={{0,192},{1,49},{16,208},{17,1},{32,224},{33,17},{48,240},{49,33},{... | collective-permute-start | bytes 1572872 | tf_op jit(solution)/shard_map/ppermute | solution.py:35
  84.6 12.6 %collective-permute-start.20 = (bf16[8,2,128,128]{3,2,1,0:T(8,128)(2,1)}, bf16[8,2,128,128]{3,2,1,0:T(8,128)(2,1)}, u32[]{:S(2)}, u32[]{:S(2)}) collective-permute-start(bf16[8,2,128,128]{3,2,1,0:T(8,128)(2,1)} %collective-permute-done.19.refs_14_), channel_id=1, source_target_pairs={{0,64},{1,17},{16,80},{17,33},{32,96},{33,49},{48,112},{49,1},{64,... | collective-permute-start | bytes 1572872 | tf_op jit(solution)/shard_map/ppermute | solution.py:35
  84.6 18.2 %collective-permute-start.22 = (bf16[8,2,128,128]{3,2,1,0:T(8,128)(2,1)}, bf16[8,2,128,128]{3,2,1,0:T(8,128)(2,1)}, u32[]{:S(2)}, u32[]{:S(2)}) collective-permute-start(bf16[8,2,128,128]{3,2,1,0:T(8,128)(2,1)} %collective-permute-done.21.refs_15_), channel_id=1, source_target_pairs={{0,64},{1,17},{16,80},{17,33},{32,96},{33,49},{48,112},{49,1},{64,... | collective-permute-start | bytes 1572872 | tf_op jit(solution)/shard_map/ppermute | solution.py:35
  115.7 14.3 %collective-permute-start = (bf16[8,2,128,128]{3,2,1,0:T(8,128)(2,1)S(1)}, bf16[8,2,128,128]{3,2,1,0:T(8,128)(2,1)S(1)}, u32[]{:S(2)}, u32[]{:S(2)}) collective-permute-start(bf16[8,2,128,128]{3,2,1,0:T(8,128)(2,1)S(1)} %get-tuple-element.20.refs_0_), channel_id=1, source_target_pairs={{0,48},{1,193},{16,0},{17,209},{32,16},{33,225},{48,32},{49,241},{... | collective-permute-start | bytes 1572872 | tf_op jit(solution)/shard_map/cond/branch_0_fun/ppermute | solution.py:35
  118.3 11.7 %collective-permute-start.1 = (bf16[8,2,128,128]{3,2,1,0:T(8,128)(2,1)S(1)}, bf16[8,2,128,128]{3,2,1,0:T(8,128)(2,1)S(1)}, u32[]{:S(2)}, u32[]{:S(2)}) collective-permute-start(bf16[8,2,128,128]{3,2,1,0:T(8,128)(2,1)S(1)} %get-tuple-element.20.refs_0_), channel_id=1, source_target_pairs={{0,32},{1,129},{16,48},{17,145},{32,0},{33,161},{48,16},{49,177},{... | collective-permute-start | bytes 1572872 | tf_op jit(solution)/shard_map/cond/branch_0_fun/ppermute | solution.py:35
  118.4 15.2 %collective-permute-start.2 = (bf16[8,2,128,128]{3,2,1,0:T(8,128)(2,1)S(1)}, bf16[8,2,128,128]{3,2,1,0:T(8,128)(2,1)S(1)}, u32[]{:S(2)}, u32[]{:S(2)}) collective-permute-start(bf16[8,2,128,128]{3,2,1,0:T(8,128)(2,1)S(1)} %get-tuple-element.20.refs_0_), channel_id=1, source_target_pairs={{0,16},{1,65},{16,32},{17,81},{32,48},{33,97},{48,0},{49,113},{64,... | collective-permute-start | bytes 1572872 | tf_op jit(solution)/shard_map/cond/branch_0_fun/ppermute | solution.py:35
  130.0 3.6 %copy-start.1 = (bf16[8,2,128,128]{3,2,1,0:T(8,128)(2,1)}, bf16[8,2,128,128]{3,2,1,0:T(8,128)(2,1)S(1)}, u32[]{:S(2)}) copy-start(bf16[8,2,128,128]{3,2,1,0:T(8,128)(2,1)S(1)} %collective-permute-done.refs_1_) | copy-start | bytes 1572868 | tf_op jit(solution)/shard_map/cond
  130.0 3.6 %copy-start.2 = (bf16[8,2,128,128]{3,2,1,0:T(8,128)(2,1)}, bf16[8,2,128,128]{3,2,1,0:T(8,128)(2,1)S(1)}, u32[]{:S(2)}) copy-start(bf16[8,2,128,128]{3,2,1,0:T(8,128)(2,1)S(1)} %collective-permute-done.1.refs_2_) | copy-start | bytes 1572868 | tf_op jit(solution)/shard_map/cond
  133.6 0.8 copy-start.3
  137.5 9.8 %collective-permute-start.3 = (bf16[8,2,128,128]{3,2,1,0:T(8,128)(2,1)}, bf16[8,2,128,128]{3,2,1,0:T(8,128)(2,1)S(1)}, u32[]{:S(2)}, u32[]{:S(2)}) collective-permute-start(bf16[8,2,128,128]{3,2,1,0:T(8,128)(2,1)} %get-tuple-element.22), channel_id=1, source_target_pairs={{0,64},{1,17},{16,80},{17,33},{32,96},{33,49},{48,112},{49,1},{64,... | collective-permute-start | bytes 1572872 | tf_op jit(solution)/shard_map/cond/branch_0_fun/ppermute | solution.py:35
  138.5 14.9 %collective-permute-start.4 = (bf16[8,2,128,128]{3,2,1,0:T(8,128)(2,1)}, bf16[8,2,128,128]{3,2,1,0:T(8,128)(2,1)S(1)}, u32[]{:S(2)}, u32[]{:S(2)}) collective-permute-start(bf16[8,2,128,128]{3,2,1,0:T(8,128)(2,1)} %get-tuple-element.23), channel_id=1, source_target_pairs={{0,128},{1,33},{16,144},{17,49},{32,160},{33,1},{48,176},{49,17},{... | collective-permute-start | bytes 1572872 | tf_op jit(solution)/shard_map/cond/branch_0_fun/ppermute | solution.py:35
  140.7 12.9 %collective-permute-start.5 = (bf16[8,2,128,128]{3,2,1,0:T(8,128)(2,1)}, bf16[8,2,128,128]{3,2,1,0:T(8,128)(2,1)S(1)}, u32[]{:S(2)}, u32[]{:S(2)}) collective-permute-start(bf16[8,2,128,128]{3,2,1,0:T(8,128)(2,1)} %get-tuple-element.24), channel_id=1, source_target_pairs={{0,192},{1,49},{16,208},{17,1},{32,224},{33,17},{48,240},{49,33},{... | collective-permute-start | bytes 1572872 | tf_op jit(solution)/shard_map/cond/branch_0_fun/ppermute | solution.py:35
  147.3 6.2 %copy-start.9 = (bf16[8,2,128,128]{3,2,1,0:T(8,128)(2,1)}, bf16[8,2,128,128]{3,2,1,0:T(8,128)(2,1)S(1)}, u32[]{:S(2)}) copy-start(bf16[8,2,128,128]{3,2,1,0:T(8,128)(2,1)S(1)} %collective-permute-done.3.refs_4_) | copy-start | bytes 1572868 | tf_op jit(solution)/shard_map/cond
  153.4 0.8 copy-start.10
  153.6 0.8 copy-start.11
  157.2 3.4 %collective-permute-start.25 = (bf16[8,128,128]{2,1,0:T(8,128)(2,1)S(1)}, bf16[8,128,128]{2,1,0:T(8,128)(2,1)S(1)}, u32[]{:S(2)}, u32[]{:S(2)}) collective-permute-start(bf16[8,128,128]{2,1,0:T(8,128)(2,1)S(1)} %get-tuple-element.48), channel_id=1, source_target_pairs={{0,1},{1,0},{2,3},{3,2},{4,5},{5,4},{6,7},{7,6},{8,9},{9,8},{10,11... | collective-permute-start | bytes 786440 | tf_op jit(solution)/shard_map/ppermute | solution.py:39
  159.4 2.0 %collective-permute-start.26 = (bf16[8,128,128]{2,1,0:T(8,128)(2,1)S(1)}, bf16[8,128,128]{2,1,0:T(8,128)(2,1)S(1)}, u32[]{:S(2)}, u32[]{:S(2)}) collective-permute-start(bf16[8,128,128]{2,1,0:T(8,128)(2,1)S(1)} %get-tuple-element.49), channel_id=1, source_target_pairs={{0,1},{1,0},{2,3},{3,2},{4,5},{5,4},{6,7},{7,6},{8,9},{9,8},{10,11... | collective-permute-start | bytes 786440 | tf_op jit(solution)/shard_map/ppermute | solution.py:39
Sparse Core Ops, SparseCore 0:
  9.8 102.4 all-gather.4
